TPU v7x, 32 devices: a whole 2x2x4 slice. The times are simulated.
32 devices in a mesh: dom: 8 (over y, x, core), sub: 4 (over z).
Axes of the slice: x: 2, y: 2, z: 4, core: 2. Of those that a mesh axis runs over, the one named last changes fastest.
Arguments:
- velocity: float32 [3, 40, 36, 128], P(None, 'dom', 'sub'), may hold values from -8 to 8, as said below
- displacement: float32 [3, 40, 36, 128], P(None, 'dom', 'sub'), may hold values from -0.02 to 0.02, as said below
- energy: float32 [8, 16, 16, 64], P(None, 'dom', 'sub'), may hold values from 0.5 to 2
- rho_weight: float32 [27, 16, 16, 64], P(None, 'dom', 'sub'), may hold values from 0.5 to 2
- mass_share: float32 [4, 16, 16, 64], P(None, 'dom', 'sub'), may hold values from 0.2 to 2
- energy_share: float32 [4, 16, 16, 64], P(None, 'dom', 'sub'), may hold values from 0.5 to 2
- material_id: int32 [16, 16, 64], P('dom', 'sub'), may hold values from 0 to 3
- mix_mask: int32 [4, 16, 16, 64], P(None, 'dom', 'sub'), may hold values 0 or 1
Outputs:
- accel: float32 [3, 40, 36, 128], P(None, 'dom', 'sub')
- residual: float32 [3, 40, 36, 128], P(None, 'dom', 'sub')
- energy_rate: float32 [8, 16, 16, 64], P(None, 'dom', 'sub')
Inputs may be any that keep to these rules, and one draw needn't show every extreme that they name: `velocity`: every copy of a grid node holds the same value. `displacement`: every copy of a grid node holds the same value.
All inputs are finite; a program needn't handle non-finite values. No bound on the sum of `mix_mask` on one device may be relied on, other than what follows from the above.
Results may differ from a plain program's by a relative error of at most 0.0003.
Values sent between devices are 32-bit elements; how exact they have to be, the bound alone decides.
A program may use at most 64 MiB of HBM per device.

v0:
```python
import math

import jax
import jax.numpy as jnp
import numpy as np
from jax import lax
from jax.sharding import PartitionSpec as P

MATS = 4
EQ_ITERS = 4
CG_ITERS = 3


gammas = (1.4, 1.67, 2.0, 3.0)
cold_terms = (0.3, 1.2, 0.6, 2.4)
highest = lax.Precision.HIGHEST


def extended(block, sides, width):
    for axis, dim in sides:
        count = lax.axis_size(axis)
        forward = [(i, i + 1) for i in range(count - 1)]
        forward.append((count - 1, 0))
        backward = [(target, source) for source, target in forward]
        low = lax.ppermute(
            lax.slice_in_dim(block, block.shape[dim] - width, None, axis=dim), axis, forward
        )
        high = lax.ppermute(lax.slice_in_dim(block, 0, width, axis=dim), axis, backward)
        block = jnp.concatenate([low, block, high], axis=dim)
    return block


def tensor_three(first, second, third):
    grid = (
        first[:, None, None, :, None, None]
        * second[None, :, None, None, :, None]
        * third[None, None, :, None, None, :]
    )
    rows = first.shape[0] * second.shape[0] * third.shape[0]
    columns = first.shape[1] * second.shape[1] * third.shape[1]
    return grid.reshape(rows, columns)


def basis_tables():
    spread_root = math.sqrt(0.15)
    points = np.array([0.5 - spread_root, 0.5, 0.5 + spread_root])
    quad_one = np.array([5.0, 8.0, 5.0]) / 18.0
    value_one = np.stack(
        [
            2.0 * (points - 0.5) * (points - 1.0),
            -4.0 * points * (points - 1.0),
            2.0 * points * (points - 0.5),
        ],
        1,
    )
    slope_one = np.stack([4.0 * points - 3.0, 4.0 - 8.0 * points, 4.0 * points - 1.0], 1)
    linear_one = np.stack([1.0 - points, points], 1)
    values = tensor_three(value_one, value_one, value_one)
    slopes = np.stack(
        [
            tensor_three(slope_one, value_one, value_one),
            tensor_three(value_one, slope_one, value_one),
            tensor_three(value_one, value_one, slope_one),
        ]
    )
    linear = tensor_three(linear_one, linear_one, linear_one)
    weights = (quad_one[:, None, None] * quad_one[None, :, None] * quad_one[None, None, :]).reshape(
        27
    )
    return (
        jnp.asarray(values, jnp.float32),
        jnp.asarray(slopes, jnp.float32),
        jnp.asarray(linear, jnp.float32),
        jnp.asarray(weights, jnp.float32),
    )


def depth_table(zone_z):
    layer = jnp.arange(2 * zone_z, dtype=jnp.int32)[:, None, None]
    offset = jnp.arange(3, dtype=jnp.int32)[None, :, None]
    zone_at = jnp.arange(zone_z, dtype=jnp.int32)[None, None, :]
    return jnp.where(layer == (2 * zone_at + offset) % (2 * zone_z), 1.0, 0.0).astype(jnp.float32)


def zone_corners(nodes_in, zone_x, zone_y, table):
    by_depth = jnp.einsum("cxyk,ksz->scxyz", nodes_in, table, precision=highest)
    pieces = []
    for shift_x in range(3):
        for shift_y in range(3):
            for shift_z in range(3):
                pieces.append(
                    by_depth[shift_z][
                        :, shift_x : shift_x + 2 * zone_x : 2, shift_y : shift_y + 2 * zone_y : 2
                    ]
                )
    return jnp.stack(pieces, 0)


def weave_axis(contrib, axis_at):
    lower_part, middle_part, upper_part = (contrib[0], contrib[1], contrib[2])
    zone_count = lower_part.shape[axis_at]
    high_pad = [(0, 0)] * lower_part.ndim
    high_pad[axis_at] = (0, 1)
    low_pad = [(0, 0)] * lower_part.ndim
    low_pad[axis_at] = (1, 0)
    even_rows = jnp.pad(lower_part, high_pad) + jnp.pad(upper_part, low_pad)
    even_head = lax.slice_in_dim(even_rows, 0, zone_count, axis=axis_at)
    even_tail = lax.slice_in_dim(even_rows, zone_count, zone_count + 1, axis=axis_at)
    woven_rows = jnp.stack([even_head, middle_part], axis_at + 1)
    extent = list(even_head.shape)
    extent[axis_at] = 2 * zone_count
    return jnp.concatenate([woven_rows.reshape(extent), even_tail], axis_at)


def place_zones(contrib, table):
    spread = contrib.reshape((3, 3, 3) + contrib.shape[1:])
    spread = weave_axis(spread, 3)
    spread = weave_axis(spread, 3)
    return jnp.einsum("scxyz,ksz->cxyk", spread, table, precision=highest)


def adjugate_of(matrix):
    cofactors = []
    for column in range(3):
        entries = []
        for line_at in range(3):
            entries.append(
                matrix[(line_at + 1) % 3, (column + 1) % 3]
                * matrix[(line_at + 2) % 3, (column + 2) % 3]
                - matrix[(line_at + 1) % 3, (column + 2) % 3]
                * matrix[(line_at + 2) % 3, (column + 1) % 3]
            )
        cofactors.append(jnp.stack(entries))
    return jnp.stack(cofactors)


def zone_force(
    displacement,
    velocity,
    energy,
    rho_weight,
    mass_share,
    energy_share,
    material_id,
    mix_mask,
    tables,
    table_z,
):
    value_table, slope_table, linear_table, weight_table = tables
    zone_x, zone_y = (energy.shape[1], energy.shape[2])
    disp_zone = zone_corners(displacement, zone_x, zone_y, table_z)
    vel_zone = zone_corners(velocity, zone_x, zone_y, table_z)
    identity = jnp.eye(3, dtype=jnp.float32)[:, :, None, None, None, None]
    jacobian = jnp.einsum("dqn,ncxyz->cdqxyz", slope_table, disp_zone, precision=highest) + identity
    velgrad = jnp.einsum("dqn,ncxyz->cdqxyz", slope_table, vel_zone, precision=highest)
    adjugate = adjugate_of(jacobian)
    determinant = jnp.sum(jacobian[0] * adjugate[:, 0], axis=0)
    density = rho_weight / determinant
    energy_points = jnp.einsum("qj,jxyz->qxyz", linear_table, energy, precision=highest)
    material = jnp.arange(MATS, dtype=jnp.int32)[:, None, None, None]
    present = jnp.where((mix_mask == 1) | (material_id[None] == material), 1.0, 0.0).astype(
        jnp.float32
    )
    weighted = present * mass_share
    mass_fraction = weighted / jnp.sum(weighted, 0, keepdims=True)
    gamma_less = jnp.asarray(gammas, jnp.float32)[:, None, None, None, None] - 1.0
    cold_part = jnp.asarray(cold_terms, jnp.float32)[:, None, None, None, None]
    pressure_load = (
        gamma_less * density[None] * (mass_fraction * energy_share)[:, None] * energy_points[None]
    )
    fraction = jnp.broadcast_to(
        (present / jnp.sum(present, 0, keepdims=True))[:, None], pressure_load.shape
    )
    for sweep_at in range(EQ_ITERS):
        grown_part = jnp.sqrt(fraction * (pressure_load + cold_part * fraction))
        fraction = grown_part / jnp.sum(grown_part, 0, keepdims=True)
    pressure = jnp.sum(pressure_load + cold_part * fraction, 0)
    stress = weight_table[:, None, None, None] * pressure
    force_zone = jnp.einsum(
        "dqn,dcqxyz->ncxyz", slope_table, adjugate * stress[None, None], precision=highest
    )
    divergence = jnp.sum(velgrad * jnp.swapaxes(adjugate, 0, 1), (0, 1))
    work_rate = jnp.einsum("qj,qxyz->jxyz", linear_table, stress * divergence, precision=highest)
    lumped = jnp.einsum(
        "qj,qxyz->jxyz",
        linear_table,
        weight_table[:, None, None, None] * rho_weight,
        precision=highest,
    )
    return (force_zone, -work_rate / lumped)


def mass_zone(node_field, mass_weight, tables, table_z):
    value_table = tables[0]
    corners = zone_corners(node_field, mass_weight.shape[1], mass_weight.shape[2], table_z)
    at_points = (
        jnp.einsum("qn,ncxyz->cqxyz", value_table, corners, precision=highest) * mass_weight[None]
    )
    return jnp.einsum("qn,cqxyz->ncxyz", value_table, at_points, precision=highest)


def assemble(local_sum):
    widened = extended(local_sum, (("dom", 1), ("sub", 2)), 1)
    middle_rows = widened[:, :, 1:-1]
    summed = local_sum.at[:, 0].add(middle_rows[:, 0]).at[:, -1].add(middle_rows[:, -1])
    lower_side = widened[:, :, 0]
    upper_side = widened[:, :, -1]
    lower_side = lower_side[:, 1:-1].at[:, 0].add(lower_side[:, 0]).at[:, -1].add(lower_side[:, -1])
    upper_side = upper_side[:, 1:-1].at[:, 0].add(upper_side[:, 0]).at[:, -1].add(upper_side[:, -1])
    return summed.at[:, :, 0].add(lower_side).at[:, :, -1].add(upper_side)


def inner_pair(left_field, right_field):
    owned_left = left_field[:, :-1, :-1]
    owned_right = right_field[:, :-1, :-1]
    return lax.psum(
        (jnp.sum(owned_left * owned_left), jnp.sum(owned_left * owned_right)), ("dom", "sub")
    )


def per_device(
    velocity, displacement, energy, rho_weight, mass_share, energy_share, material_id, mix_mask
):
    tables = basis_tables()
    table_z = depth_table(energy.shape[3])
    force_zone, energy_rate = zone_force(
        displacement,
        velocity,
        energy,
        rho_weight,
        mass_share,
        energy_share,
        material_id,
        mix_mask,
        tables,
        table_z,
    )
    force_total = assemble(place_zones(force_zone, table_z))
    mass_weight = tables[3][:, None, None, None] * rho_weight

    def apply_mass(node_field):
        return assemble(place_zones(mass_zone(node_field, mass_weight, tables, table_z), table_z))

    solution = jnp.zeros_like(force_total)
    residual = force_total
    mapped = apply_mass(residual)
    direction = jnp.zeros_like(force_total)
    direction_image = jnp.zeros_like(force_total)
    image_image = jnp.zeros_like(force_total)
    norm_old = 1.0
    step_old = 1.0
    for sweep_at in range(CG_ITERS):
        norm_now, product = inner_pair(residual, mapped)
        if sweep_at + 1 < CG_ITERS:
            mapped_twice = apply_mass(mapped)
        if sweep_at == 0:
            growth = 0.0
            step_size = norm_now / product
        else:
            growth = norm_now / norm_old
            step_size = norm_now / (product - growth * norm_now / step_old)
        direction = residual + growth * direction
        direction_image = mapped + growth * direction_image
        solution = solution + step_size * direction
        residual = residual - step_size * direction_image
        if sweep_at + 1 < CG_ITERS:
            image_image = mapped_twice + growth * image_image
            mapped = mapped - step_size * image_image
        norm_old = norm_now
        step_old = step_size
    return (solution, residual, energy_rate)


def solution(mesh):
    placed = (
        P(None, "dom", "sub", None),
        P(None, "dom", "sub", None),
        P(None, "dom", "sub", None),
        P(None, "dom", "sub", None),
        P(None, "dom", "sub", None),
        P(None, "dom", "sub", None),
        P("dom", "sub", None),
        P(None, "dom", "sub", None),
    )
    return jax.shard_map(
        per_device,
        mesh=mesh,
        in_specs=placed,
        out_specs=(
            P(None, "dom", "sub", None),
            P(None, "dom", "sub", None),
            P(None, "dom", "sub", None),
        ),
        check_vma=False,
    )
```

profile of v0, /device:TPU:0, one launch (start us, length us, event | category | flops | bytes accessed | tf_op | source)
XLA Modules:
  0.0 234.0 jit_solution(1128196843628028064)
XLA Ops:
  0.7 1.4 convolution_bitcast_fusion.9
  7.9 1.1 fusion
  9.3 0.7 copy-done.4
  18.4 0.8 fusion.29
  19.2 1.2 fusion.77
  20.4 1.5 fusion.153
  21.9 1.6 add_reduce_fusion
  23.8 1.1 fusion.2
  25.2 0.8 convolution_bitcast_fusion.4
  27.7 4.3 %collective-permute-done = f32[3,1,9,128]{3,1,0,2:T(1,128)S(1)} collective-permute-done((f32[3,1,9,128]{3,1,0,2:T(1,128)S(1)}, f32[3,1,9,128]{3,1,0,2:T(1,128)S(1)}, u32[]{:S(2)}, u32[]{:S(2)}) %collective-permute-start) | collective-permute-done | bytes 13856 | tf_op jit(solution)/shard_map/ppermute | solution.py:25
  32.2 1.3 collective-permute-done.1
  33.5 4.4 %collective-permute-start.3 = (f32[3,7,1,128]{3,2,1,0:T(1,128)S(1)}, f32[3,7,1,128]{3,2,1,0:T(1,128)S(1)}, u32[]{:S(2)}, u32[]{:S(2)}) collective-permute-start(f32[3,7,1,128]{3,2,1,0:T(1,128)S(1)} %get-tuple-element.463), channel_id=1, source_target_pairs={{1,0},{2,1},{3,2},{0,3},{5,4},{6,5},{7,6},{4,7},{9,8},{10,9},{11,1... | collective-permute-start | bytes 32264 | tf_op jit(solution)/shard_map/ppermute | solution.py:28
  38.1 1.3 collective-permute-done.3
  39.4 4.1 %collective-permute-done.2 = f32[3,7,1,128]{3,1,0,2:T(8,128)S(1)} collective-permute-done((f32[3,7,1,128]{3,1,0,2:T(8,128)S(1)}, f32[3,7,1,128]{3,1,0,2:T(8,128)S(1)}, u32[]{:S(2)}, u32[]{:S(2)}) %collective-permute-start.2) | collective-permute-done | bytes 10784 | tf_op jit(solution)/shard_map/ppermute | solution.py:25
  52.7 4.0 %collective-permute-done.4 = f32[3,1,9,128]{3,1,0,2:T(1,128)S(1)} collective-permute-done((f32[3,1,9,128]{3,1,0,2:T(1,128)S(1)}, f32[3,1,9,128]{3,1,0,2:T(1,128)S(1)}, u32[]{:S(2)}, u32[]{:S(2)}) %collective-permute-start.4) | collective-permute-done | bytes 13856 | tf_op jit(solution)/shard_map/ppermute | solution.py:25
  56.8 1.4 collective-permute-done.5
  58.3 2.0 collective-permute-start.6
  60.5 1.5 collective-permute-done.7
  62.0 1.9 collective-permute-done.6
  73.0 3.8 %collective-permute-done.8 = f32[3,1,9,128]{3,1,0,2:T(1,128)S(1)} collective-permute-done((f32[3,1,9,128]{3,1,0,2:T(1,128)S(1)}, f32[3,1,9,128]{3,1,0,2:T(1,128)S(1)}, u32[]{:S(2)}, u32[]{:S(2)}) %collective-permute-start.8) | collective-permute-done | bytes 13856 | tf_op jit(solution)/shard_map/ppermute | solution.py:25
  77.5 38.1 %all-reduce.18 = (f32[]{:T(128)}, f32[]{:T(128)}) all-reduce(f32[]{:T(128)} %get-tuple-element.404, f32[]{:T(128)} %get-tuple-element.403), channel_id=1, replica_groups=mesh['dom'=8,'sub'=4] {'dom','sub'}, use_global_device_ids=true, to_apply=%region_9.10 | all-reduce | flops 2 | bytes 16 | tf_op jit(solution)/shard_map/psum | solution.py:216
  117.0 1.6 collective-permute-start.11
  119.3 1.5 collective-permute-done.11
  120.8 3.3 %collective-permute-done.10 = f32[3,7,1,128]{3,1,0,2:T(8,128)S(1)} collective-permute-done((f32[3,7,1,128]{3,1,0,2:T(8,128)S(1)}, f32[3,7,1,128]{3,1,0,2:T(8,128)S(1)}, u32[]{:S(2)}, u32[]{:S(2)}) %collective-permute-start.10) | collective-permute-done | bytes 10784 | tf_op jit(solution)/shard_map/ppermute | solution.py:25
  134.2 3.2 %collective-permute-done.12 = f32[3,1,9,128]{3,1,0,2:T(1,128)S(1)} collective-permute-done((f32[3,1,9,128]{3,1,0,2:T(1,128)S(1)}, f32[3,1,9,128]{3,1,0,2:T(1,128)S(1)}, u32[]{:S(2)}, u32[]{:S(2)}) %collective-permute-start.12) | collective-permute-done | bytes 13856 | tf_op jit(solution)/shard_map/ppermute | solution.py:25
  137.7 0.7 fusion.79
  138.4 38.0 %all-reduce.17 = (f32[]{:T(128)}, f32[]{:T(128)}) all-reduce(f32[]{:T(128)} %get-tuple-element.402, f32[]{:T(128)} %get-tuple-element.401), channel_id=1, replica_groups=mesh['dom'=8,'sub'=4] {'dom','sub'}, use_global_device_ids=true, to_apply=%region_13.14 | all-reduce | flops 2 | bytes 16 | tf_op jit(solution)/shard_map/psum | solution.py:216
  180.8 2.3 collective-permute-start.15
  183.9 1.4 collective-permute-done.15
  185.4 3.2 %collective-permute-done.14 = f32[3,7,1,128]{3,1,0,2:T(8,128)S(1)} collective-permute-done((f32[3,7,1,128]{3,1,0,2:T(8,128)S(1)}, f32[3,7,1,128]{3,1,0,2:T(8,128)S(1)}, u32[]{:S(2)}, u32[]{:S(2)}) %collective-permute-start.14) | collective-permute-done | bytes 10784 | tf_op jit(solution)/shard_map/ppermute | solution.py:25
  189.5 39.3 %all-reduce.16 = (f32[]{:T(128)}, f32[]{:T(128)}) all-reduce(f32[]{:T(128)} %get-tuple-element.400, f32[]{:T(128)} %get-tuple-element.399), channel_id=1, replica_groups=mesh['dom'=8,'sub'=4] {'dom','sub'}, use_global_device_ids=true, to_apply=%region_17.18 | all-reduce | flops 2 | bytes 16 | tf_op jit(solution)/shard_map/psum | solution.py:216
  232.7 0.7 copy.358
  (489 shorter events, 47.4 us)
Async XLA Ops:
  0.6 16.7 %copy-start = (f32[8,2,4,64]{3,2,1,0:T(4,128)S(1)}, f32[8,2,4,64]{3,2,1,0:T(4,128)}, u32[]{:S(2)}) copy-start(f32[8,2,4,64]{3,2,1,0:T(4,128)} %param.80) | copy-start | bytes 49156
  0.7 7.3 %copy-start.3 = (f32[3,27,27,1,1,1]{2,1,0,5,4,3:T(8,128)S(1)}, f32[3,27,27,1,1,1]{2,1,0,5,4,3:T(8,128)}, u32[]{:S(2)}) copy-start(f32[3,27,27,1,1,1]{2,1,0,5,4,3:T(8,128)} %constant.789) | copy-start | bytes 26248
  9.1 0.9 copy-start.4
  16.3 0.9 copy-start.2
  16.5 0.9 copy-start.6
  16.5 1.3 copy-start.5
  16.5 1.3 copy-start.7
  16.5 1.2 copy-start.11
  16.5 1.3 copy-start.8
  16.5 1.3 copy-start.9
  16.6 1.3 copy-start.10
  23.6 1.3 copy-start.12
  27.2 4.8 %collective-permute-start = (f32[3,1,9,128]{3,1,0,2:T(1,128)S(1)}, f32[3,1,9,128]{3,1,0,2:T(1,128)S(1)}, u32[]{:S(2)}, u32[]{:S(2)}) collective-permute-start(f32[3,1,9,128]{3,1,0,2:T(1,128)S(1)} %slice.1985), channel_id=1, source_target_pairs={{0,4},{4,8},{8,12},{12,16},{16,20},{20,24},{24,28},{28,0},{1,5},{5... | collective-permute-start | bytes 41480 | tf_op jit(solution)/shard_map/ppermute | solution.py:25
  32.0 1.5 collective-permute-start.1
  33.5 5.8 %collective-permute-start.3 = (f32[3,7,1,128]{3,2,1,0:T(1,128)S(1)}, f32[3,7,1,128]{3,2,1,0:T(1,128)S(1)}, u32[]{:S(2)}, u32[]{:S(2)}) collective-permute-start(f32[3,7,1,128]{3,2,1,0:T(1,128)S(1)} %get-tuple-element.463), channel_id=1, source_target_pairs={{1,0},{2,1},{3,2},{0,3},{5,4},{6,5},{7,6},{4,7},{9,8},{10,9},{11,1... | collective-permute-start | bytes 32264 | tf_op jit(solution)/shard_map/ppermute | solution.py:28
  37.9 5.5 %collective-permute-start.2 = (f32[3,7,1,128]{3,1,0,2:T(8,128)S(1)}, f32[3,7,1,128]{3,1,0,2:T(8,128)S(1)}, u32[]{:S(2)}, u32[]{:S(2)}) collective-permute-start(f32[3,7,1,128]{3,1,0,2:T(8,128)S(1)} %copy.395), channel_id=1, source_target_pairs={{0,1},{1,2},{2,3},{3,0},{4,5},{5,6},{6,7},{7,4},{8,9},{9,10},{10,1... | collective-permute-start | bytes 32264 | tf_op jit(solution)/shard_map/ppermute | solution.py:25
  43.7 6.6 %copy-start.1 = (f32[27,27,1,1,1]{1,0,4,3,2:T(8,128)S(1)}, f32[27,27,1,1,1]{1,0,4,3,2:T(8,128)}, u32[]{:S(2)}) copy-start(f32[27,27,1,1,1]{1,0,4,3,2:T(8,128)} %constant.791) | copy-start | bytes 8752
  52.6 4.1 %collective-permute-start.4 = (f32[3,1,9,128]{3,1,0,2:T(1,128)S(1)}, f32[3,1,9,128]{3,1,0,2:T(1,128)S(1)}, u32[]{:S(2)}, u32[]{:S(2)}) collective-permute-start(f32[3,1,9,128]{3,1,0,2:T(1,128)S(1)} %slice.2015), channel_id=1, source_target_pairs={{0,4},{4,8},{8,12},{12,16},{16,20},{20,24},{24,28},{28,0},{1,5},{5... | collective-permute-start | bytes 41480 | tf_op jit(solution)/shard_map/ppermute | solution.py:25
  56.7 1.5 collective-permute-start.5
  58.2 3.7 %collective-permute-start.7 = (f32[3,7,1,128]{3,1,0,2:T(8,128)S(1)}, f32[3,7,1,128]{3,1,0,2:T(8,128)S(1)}, u32[]{:S(2)}, u32[]{:S(2)}) collective-permute-start(f32[3,7,1,128]{3,1,0,2:T(8,128)S(1)} %get-tuple-element.469), channel_id=1, source_target_pairs={{1,0},{2,1},{3,2},{0,3},{5,4},{6,5},{7,6},{4,7},{9,8},{10,9},{11,1... | collective-permute-start | bytes 32264 | tf_op jit(solution)/shard_map/ppermute | solution.py:28
  58.3 5.5 %collective-permute-start.6 = (f32[3,7,1,128]{3,1,0,2:T(8,128)S(1)}, f32[3,7,1,128]{3,1,0,2:T(8,128)S(1)}, u32[]{:S(2)}, u32[]{:S(2)}) collective-permute-start(f32[3,7,1,128]{3,1,0,2:T(8,128)S(1)} %get-tuple-element.470), channel_id=1, source_target_pairs={{0,1},{1,2},{2,3},{3,0},{4,5},{5,6},{6,7},{7,4},{8,9},{9,10},{10,1... | collective-permute-start | bytes 32264 | tf_op jit(solution)/shard_map/ppermute | solution.py:25
  72.7 4.1 %collective-permute-start.8 = (f32[3,1,9,128]{3,1,0,2:T(1,128)S(1)}, f32[3,1,9,128]{3,1,0,2:T(1,128)S(1)}, u32[]{:S(2)}, u32[]{:S(2)}) collective-permute-start(f32[3,1,9,128]{3,1,0,2:T(1,128)S(1)} %slice.2046), channel_id=1, source_target_pairs={{0,4},{4,8},{8,12},{12,16},{16,20},{20,24},{24,28},{28,0},{1,5},{5... | collective-permute-start | bytes 41480 | tf_op jit(solution)/shard_map/ppermute | solution.py:25
  76.8 40.2 %collective-permute-start.9 = (f32[3,1,9,128]{3,1,0,2:T(1,128)S(1)}, f32[3,1,9,128]{3,1,0,2:T(1,128)S(1)}, u32[]{:S(2)}, u32[]{:S(2)}) collective-permute-start(f32[3,1,9,128]{3,1,0,2:T(1,128)S(1)} %get-tuple-element.479), channel_id=1, source_target_pairs={{4,0},{8,4},{12,8},{16,12},{20,16},{24,20},{28,24},{0,28},{5,1},{9... | collective-permute-start | bytes 41480 | tf_op jit(solution)/shard_map/ppermute | solution.py:28
  117.0 3.7 %collective-permute-start.11 = (f32[3,7,1,128]{3,1,0,2:T(8,128)S(1)}, f32[3,7,1,128]{3,1,0,2:T(8,128)S(1)}, u32[]{:S(2)}, u32[]{:S(2)}) collective-permute-start(f32[3,7,1,128]{3,1,0,2:T(8,128)S(1)} %get-tuple-element.467), channel_id=1, source_target_pairs={{1,0},{2,1},{3,2},{0,3},{5,4},{6,5},{7,6},{4,7},{9,8},{10,9},{11,1... | collective-permute-start | bytes 32264 | tf_op jit(solution)/shard_map/ppermute | solution.py:28
  118.6 5.5 %collective-permute-start.10 = (f32[3,7,1,128]{3,1,0,2:T(8,128)S(1)}, f32[3,7,1,128]{3,1,0,2:T(8,128)S(1)}, u32[]{:S(2)}, u32[]{:S(2)}) collective-permute-start(f32[3,7,1,128]{3,1,0,2:T(8,128)S(1)} %get-tuple-element.468), channel_id=1, source_target_pairs={{0,1},{1,2},{2,3},{3,0},{4,5},{5,6},{6,7},{7,4},{8,9},{9,10},{10,1... | collective-permute-start | bytes 32264 | tf_op jit(solution)/shard_map/ppermute | solution.py:25
  133.3 4.1 %collective-permute-start.12 = (f32[3,1,9,128]{3,1,0,2:T(1,128)S(1)}, f32[3,1,9,128]{3,1,0,2:T(1,128)S(1)}, u32[]{:S(2)}, u32[]{:S(2)}) collective-permute-start(f32[3,1,9,128]{3,1,0,2:T(1,128)S(1)} %slice.2077), channel_id=1, source_target_pairs={{0,4},{4,8},{8,12},{12,16},{16,20},{20,24},{24,28},{28,0},{1,5},{5... | collective-permute-start | bytes 41480 | tf_op jit(solution)/shard_map/ppermute | solution.py:25
  137.4 43.3 %collective-permute-start.13 = (f32[3,1,9,128]{3,1,0,2:T(1,128)S(1)}, f32[3,1,9,128]{3,1,0,2:T(1,128)S(1)}, u32[]{:S(2)}, u32[]{:S(2)}) collective-permute-start(f32[3,1,9,128]{3,1,0,2:T(1,128)S(1)} %get-tuple-element.477), channel_id=1, source_target_pairs={{4,0},{8,4},{12,8},{16,12},{20,16},{24,20},{28,24},{0,28},{5,1},{9... | collective-permute-start | bytes 41480 | tf_op jit(solution)/shard_map/ppermute | solution.py:28
  180.8 4.6 %collective-permute-start.15 = (f32[3,7,1,128]{3,1,0,2:T(8,128)S(1)}, f32[3,7,1,128]{3,1,0,2:T(8,128)S(1)}, u32[]{:S(2)}, u32[]{:S(2)}) collective-permute-start(f32[3,7,1,128]{3,1,0,2:T(8,128)S(1)} %get-tuple-element.465), channel_id=1, source_target_pairs={{1,0},{2,1},{3,2},{0,3},{5,4},{6,5},{7,6},{4,7},{9,8},{10,9},{11,1... | collective-permute-start | bytes 32264 | tf_op jit(solution)/shard_map/ppermute | solution.py:28
  183.1 5.5 %collective-permute-start.14 = (f32[3,7,1,128]{3,1,0,2:T(8,128)S(1)}, f32[3,7,1,128]{3,1,0,2:T(8,128)S(1)}, u32[]{:S(2)}, u32[]{:S(2)}) collective-permute-start(f32[3,7,1,128]{3,1,0,2:T(8,128)S(1)} %get-tuple-element.466), channel_id=1, source_target_pairs={{0,1},{1,2},{2,3},{3,0},{4,5},{5,6},{6,7},{7,4},{8,9},{9,10},{10,1... | collective-permute-start | bytes 32264 | tf_op jit(solution)/shard_map/ppermute | solution.py:25
where the time goes:
time: 235 us; the launch traced here: 234 us
  blocking collectives  115 us (49%)
  waiting for transfers between devices  36.1 us (15%)
  local copies, waits for them, and re-layouts  34.3 us (15%)
  between operations  13.2 us (6%)
  starting transfers between devices  12.6 us (5%)
  matrix products  12.2 us (5%)
  other arithmetic  10.3 us (4%)
    psum x3, blocking collectives, inner_pair(): lax.psum((jnp.sum(owned_left * owned_left), jnp.sum(owned_left * owned_ri...  115 us
    ppermute x8, waiting for transfers between devices, extended(): lax.ppermute(lax.slice_in_dim(block, block.shape[dim] - width, None, axis...  27.8 us
    slice x135, local copies, waits for them, and re-layouts, zone_corners(): by_depth[shift_z]  26.6 us
    ppermute x8, starting transfers between devices, extended(): lax.ppermute(lax.slice_in_dim(block, 0, width, axis=dim), axis, backward)  8.82 us
    ppermute x8, waiting for transfers between devices, extended(): lax.ppermute(lax.slice_in_dim(block, 0, width, axis=dim), axis, backward)  8.33 us
  transfers between devices with their start and end apart: 16, of which 14 were waited for; matrix products, arithmetic and copies ran while one was open for 1% of the time, Pallas kernels for 0%

commit v1 on v0

v1 whole, which is shorter than its diff:
```python
import functools
import math

import jax
import jax.numpy as jnp
import numpy as np
from jax import lax
from jax.experimental import pallas as pl
from jax.experimental.pallas import tpu as pltpu
from jax.sharding import PartitionSpec as P
import ml_dtypes

MESH = pl.DeviceIdType.MESH
MATS = 4
EQ_ITERS = 4
CG_ITERS = 3
ROUNDS = CG_ITERS + 1

gammas = (1.4, 1.67, 2.0, 3.0)
cold_terms = (0.3, 1.2, 0.6, 2.4)

spread_root = math.sqrt(0.15)
points = np.array([0.5 - spread_root, 0.5, 0.5 + spread_root])
quad_one = np.array([5.0, 8.0, 5.0]) / 18.0
value_one = np.stack(
    [
        2.0 * (points - 0.5) * (points - 1.0),
        -4.0 * points * (points - 1.0),
        2.0 * points * (points - 0.5),
    ],
    1,
)
slope_one = np.stack([4.0 * points - 3.0, 4.0 - 8.0 * points, 4.0 * points - 1.0], 1)
linear_one = np.stack([1.0 - points, points], 1)


def round_up(value, step):
    return -(-value // step) * step


def split_table(table, axis):
    table = table.astype(np.float32)
    high = table.astype(ml_dtypes.bfloat16)
    low = (table - high.astype(np.float32)).astype(ml_dtypes.bfloat16)
    return np.concatenate([high, high, low], axis)


def depth_matrix(one, zone_z, lanes):
    table = np.zeros((2 * zone_z, lanes))
    for q in range(3):
        for z in range(zone_z):
            for k in range(3):
                table[(2 * z + k) % (2 * zone_z), q * zone_z + z] += one[q, k]
    return table


def plane_matrix(one_x, one_y, zone_x, zone_y, pad_y):
    table = np.zeros((9 * zone_x * zone_y, (2 * zone_x + 1) * pad_y))
    for a in range(3):
        for b in range(3):
            for x in range(zone_x):
                for y in range(zone_y):
                    row = ((a * 3 + b) * zone_x + x) * zone_y + y
                    for i in range(3):
                        for j in range(3):
                            table[row, (2 * x + i) * pad_y + 2 * y + j] = one_x[a, i] * one_y[b, j]
    return table


def with_faces(table, zone_x, zone_y, pad_y, pad_x):
    rows = table.T
    faces = np.zeros((2, pad_x, rows.shape[1]))
    for x in range(2 * zone_x + 1):
        faces[0, x] = rows[x * pad_y]
        faces[1, x] = rows[x * pad_y + 2 * zone_y]
    return np.concatenate([rows, faces[0], faces[1]], 0)


def split_lanes(x):
    high = x.astype(jnp.bfloat16)
    low = (x - high.astype(jnp.float32)).astype(jnp.bfloat16)
    return jnp.concatenate([high, low, high], axis=1)


def split_rows(x):
    high = x.astype(jnp.bfloat16).astype(jnp.float32)
    return jnp.concatenate([high, x - high, high], axis=0).astype(jnp.bfloat16)


def product(left, right):
    return jnp.dot(left, right, preferred_element_type=jnp.float32)


def lanes_of(x, rows):
    return jnp.concatenate([x[c * rows : (c + 1) * rows] for c in range(3)], axis=1)


def rows_of(x, lanes):
    return jnp.concatenate([x[:, c * lanes : (c + 1) * lanes] for c in range(3)], axis=0)


def kernel(
    dims,
    velocity,
    displacement,
    energy,
    rho_weight,
    mass_share,
    energy_share,
    material_id,
    mix_mask,
    depth_value,
    depth_slope,
    depth_value_t,
    depth_both_t,
    plane_value,
    plane_slopes,
    plane_value_t,
    plane_slopes_t,
    weight_table,
    accel,
    residual,
    energy_rate,
    field,
    rho,
    zone_in,
    jac,
    stress,
    part,
    total,
    face_x,
    face_y,
    corner,
    dom_parts,
    sub_parts,
    halo_send,
    halo_recv,
    dom_send,
    dom_recv,
    sub_send,
    sub_recv,
):
    n_dom, n_sub, zone_x, zone_y, zone_z, pad_x, pad_y, lanes = dims
    node_x, node_y = 2 * zone_x + 1, 2 * zone_y + 1
    plane = node_x * pad_y
    tile = zone_x * zone_y
    wide = 9 * tile
    me_dom, me_sub = lax.axis_index("dom"), lax.axis_index("sub")

    def at(shift_dom, shift_sub):
        return (lax.rem(me_dom + shift_dom + n_dom, n_dom), lax.rem(me_sub + shift_sub + n_sub, n_sub))

    corners = [(-1, -1), (-1, 1), (1, -1), (1, 1)]
    others = [at(k, 0) for k in range(1, n_dom)] + [at(0, k) for k in range(1, n_sub)]
    others += [at(dx, dy) for dx, dy in corners]
    barrier = pltpu.get_barrier_semaphore()
    for other in others:
        pl.semaphore_signal(barrier, inc=1, device_id=other, device_id_type=MESH)

    field[...] = jnp.zeros_like(field)
    for x in range(node_x):
        field[0, :, x * pad_y : x * pad_y + node_y, :] = displacement[:, x]
        field[1, :, x * pad_y : x * pad_y + node_y, :] = velocity[:, x]
    for t in range(9):
        for q in range(4):
            for x in range(zone_x):
                rho[t * tile + x * zone_y : t * tile + (x + 1) * zone_y, q * zone_z : (q + 1) * zone_z] = (
                    rho_weight[3 * t + q % 3, x]
                )
    for half in range(2):
        cols = slice(half * zone_z, (half + 1) * zone_z)
        for x in range(zone_x):
            rows = slice(x * zone_y, (x + 1) * zone_y)
            for m in range(MATS):
                present = jnp.where((mix_mask[m, x] == 1) | (material_id[x] == m), 1.0, 0.0)
                zone_in[m, rows, cols] = present
                zone_in[MATS + m, rows, cols] = mass_share[m, x]
                zone_in[2 * MATS + m, rows, cols] = energy_share[m, x]
            for j in range(8):
                zone_in[3 * MATS + j, rows, cols] = energy[j, x]

    def gradients(which):
        source = split_lanes(field[which].reshape(3 * plane, 2 * zone_z))
        by_value = split_rows(lanes_of(product(source, depth_value[...]), plane))
        by_slope = split_rows(lanes_of(product(source, depth_slope[...]), plane))
        along_xy = product(plane_slopes[...], by_value)
        along_z = product(plane_value[...], by_slope)
        jac[0] = along_xy[:wide]
        jac[1] = along_xy[wide:]
        jac[2] = along_z

    gradients(0)

    present = [zone_in[m] for m in range(MATS)]
    weighted = [present[m] * zone_in[MATS + m] for m in range(MATS)]
    weighted_sum = 1.0 / (weighted[0] + weighted[1] + weighted[2] + weighted[3])
    present_sum = 1.0 / (present[0] + present[1] + present[2] + present[3])

    def spread(x):
        return jnp.concatenate([jnp.concatenate([x, x], axis=1)] * 3, axis=0)

    start = [spread(present[m] * present_sum) for m in range(MATS)]
    load = [
        spread((gammas[m] - 1.0) * (weighted[m] * weighted_sum) * zone_in[2 * MATS + m])
        for m in range(MATS)
    ]
    lane_at = lax.broadcasted_iota(jnp.int32, (tile, lanes), 1) // zone_z
    upper = jnp.where(lane_at == 1, points[1], jnp.where(lane_at == 2, points[2], points[0])).astype(
        jnp.float32
    )
    along = []
    for j in range(4):
        low, high = zone_in[3 * MATS + 2 * j], zone_in[3 * MATS + 2 * j + 1]
        low, high = jnp.concatenate([low, low], axis=1), jnp.concatenate([high, high], axis=1)
        along.append(low + upper * (high - low))

    for a in range(3):
        rows = slice(a * 3 * tile, (a + 1) * 3 * tile)
        x_low = [linear_one[a, 0] * along[jy] + linear_one[a, 1] * along[2 + jy] for jy in range(2)]
        energy_points = jnp.concatenate(
            [linear_one[b, 0] * x_low[0] + linear_one[b, 1] * x_low[1] for b in range(3)], axis=0
        )

        def entry(c, d):
            value = jac[d, rows, c * lanes : (c + 1) * lanes]
            return value + 1.0 if c == d else value

        matrix = [[entry(c, d) for d in range(3)] for c in range(3)]
        adjugate = [[None] * 3 for _ in range(3)]
        for d in range(3):
            for c in range(3):
                adjugate[d][c] = (
                    matrix[(c + 1) % 3][(d + 1) % 3] * matrix[(c + 2) % 3][(d + 2) % 3]
                    - matrix[(c + 1) % 3][(d + 2) % 3] * matrix[(c + 2) % 3][(d + 1) % 3]
                )
        determinant = (
            matrix[0][0] * adjugate[0][0]
            + matrix[0][1] * adjugate[1][0]
            + matrix[0][2] * adjugate[2][0]
        )
        base = rho[rows, :] / determinant * energy_points
        pressure_load = [load[m] * base for m in range(MATS)]
        fraction = list(start)
        for sweep in range(EQ_ITERS):
            grown = []
            for m in range(MATS):
                square = fraction[m] * (pressure_load[m] + cold_terms[m] * fraction[m])
                grown.append(square * lax.rsqrt(jnp.maximum(square, 1e-30)))
            scale = 1.0 / ((grown[0] + grown[1]) + (grown[2] + grown[3]))
            fraction = [grown[m] * scale for m in range(MATS)]
        pressure = (
            (pressure_load[0] + cold_terms[0] * fraction[0])
            + (pressure_load[1] + cold_terms[1] * fraction[1])
            + (pressure_load[2] + cold_terms[2] * fraction[2])
            + (pressure_load[3] + cold_terms[3] * fraction[3])
        )
        weighted_pressure = weight_table[rows, :] * pressure
        for d in range(3):
            for c in range(3):
                stress[d, rows, c * lanes : (c + 1) * lanes] = weighted_pressure * adjugate[d][c]

    sends = []

    def send(source, target, to, send_sem, recv_sem):
        copy = pltpu.make_async_remote_copy(
            src_ref=source,
            dst_ref=target,
            send_sem=send_sem,
            recv_sem=recv_sem,
            device_id=to,
            device_id_type=MESH,
        )
        copy.start()
        sends.append(copy)
        return copy

    def start_halo(turn):
        copies = []
        faces_at = (plane, plane + pad_x)
        for k, dx in enumerate((-1, 1)):
            first = 0 if dx < 0 else (node_x - 1) * pad_y
            copies.append(
                send(
                    part.at[turn, :, pl.ds(first, pad_y), :],
                    face_x.at[turn, k],
                    at(dx, 0),
                    halo_send.at[turn, k],
                    halo_recv.at[turn, k],
                )
            )
        for k, dy in enumerate((-1, 1)):
            copies.append(
                send(
                    part.at[turn, :, pl.ds(faces_at[k], pad_x), :],
                    face_y.at[turn, k],
                    at(0, dy),
                    halo_send.at[turn, 2 + k],
                    halo_recv.at[turn, 2 + k],
                )
            )
        for k, (dx, dy) in enumerate(corners):
            copies.append(
                send(
                    part.at[turn, :, pl.ds(faces_at[0 if dy < 0 else 1], pad_x), :],
                    corner.at[turn, k],
                    at(dx, dy),
                    halo_send.at[turn, 4 + k],
                    halo_recv.at[turn, 4 + k],
                )
            )
        return copies

    row_at = lax.broadcasted_iota(jnp.int32, (3, pad_y, 2 * zone_z), 1)

    def finish_halo(turn, copies):
        for copy in copies:
            copy.wait_recv()
        last = node_x - 1
        for x in range(node_x):
            block = part[turn, :, x * pad_y : (x + 1) * pad_y, :]
            low = face_y[turn, 1, :, x : x + 1, :]
            high = face_y[turn, 0, :, x : x + 1, :]
            if x == 0:
                block = block + face_x[turn, 1]
                low = low + corner[turn, 3, :, last : last + 1, :]
                high = high + corner[turn, 2, :, last : last + 1, :]
            if x == last:
                block = block + face_x[turn, 0]
                low = low + corner[turn, 1, :, 0:1, :]
                high = high + corner[turn, 0, :, 0:1, :]
            block = block + jnp.where(row_at == 0, low, jnp.where(row_at == node_y - 1, high, 0.0))
            total[turn, :, x * pad_y : (x + 1) * pad_y, :] = block

    def owned(turn):
        return [
            total[turn, c, x * pad_y : x * pad_y + 2 * zone_y, :]
            for c in range(3)
            for x in range(2 * zone_x)
        ]

    def moment(left, right):
        terms = [a * b for a, b in zip(owned(left), owned(right))]
        while len(terms) > 1:
            terms = [sum(terms[k : k + 2]) for k in range(0, len(terms), 2)]
        return jnp.sum(terms[0], axis=0, keepdims=True)

    side_xy = product(
        plane_slopes_t[...],
        split_rows(jnp.concatenate([stress[0], stress[1]], axis=0)),
    )
    side_z = product(plane_value_t[...], split_rows(stress[2]))
    rows_part = plane + 2 * pad_x
    both = jnp.concatenate([rows_of(side_xy, lanes), rows_of(side_z, lanes)], axis=1)
    part[0] = product(split_lanes(both), depth_both_t[...]).reshape(3, rows_part, 2 * zone_z)
    pl.semaphore_wait(barrier, len(others))
    copies = start_halo(0)

    mass_weight = weight_table[...] * rho[...]
    gradients(1)
    work = jnp.zeros((wide, lanes), jnp.float32)
    for c in range(3):
        for d in range(3):
            work = work + jac[d, :, c * lanes : (c + 1) * lanes] * stress[d, :, c * lanes : (c + 1) * lanes]

    def to_linear(x):
        results = []
        for jx in range(2):
            for jy in range(2):
                acc = jnp.zeros((tile, lanes), jnp.float32)
                for a in range(3):
                    for b in range(3):
                        t = a * 3 + b
                        acc = acc + float(linear_one[a, jx] * linear_one[b, jy]) * x[t * tile : (t + 1) * tile]
                for jz in range(2):
                    scaled = acc * (upper if jz else 1.0 - upper)
                    folded = scaled[:, : 2 * zone_z] + scaled[:, 2 * zone_z :]
                    results.append(folded + pltpu.roll(folded, zone_z, 1))
        return results

    rates = to_linear(work)
    lumped = to_linear(mass_weight)
    for j in range(8):
        rate = -rates[j] / lumped[j]
        for x in range(zone_x):
            energy_rate[j, x] = rate[x * zone_y : (x + 1) * zone_y, :zone_z]

    finish_halo(0, copies)
    moments = [moment(0, 0)]
    weight_three = jnp.concatenate([mass_weight] * 3, axis=1)
    for turn in range(1, ROUNDS):
        source = split_lanes(total[turn - 1].reshape(3 * plane, 2 * zone_z))
        nodes = split_rows(lanes_of(product(source, depth_value[...]), plane))
        at_points = product(plane_value[...], nodes) * weight_three
        back = product(plane_value_t[...], split_rows(at_points))
        part[turn] = product(split_lanes(rows_of(back, lanes)), depth_value_t[...]).reshape(
            3, rows_part, 2 * zone_z
        )
        copies = start_halo(turn)
        if turn > 1:
            moments += [moment(turn - 2, turn - 1), moment(turn - 1, turn - 1)]
        finish_halo(turn, copies)
    moments.append(moment(ROUNDS - 2, ROUNDS - 1))

    fill = jnp.zeros((8 - len(moments), 2 * zone_z), jnp.float32)
    dom_parts[0] = jnp.concatenate(moments + [fill], axis=0)
    copies = [
        send(dom_parts.at[0], dom_parts.at[k], at(k, 0), dom_send.at[k], dom_recv.at[k])
        for k in range(1, n_dom)
    ]
    for copy in copies:
        copy.wait_recv()
    sub_parts[0] = jnp.sum(dom_parts[...], axis=0)
    copies = [
        send(sub_parts.at[0], sub_parts.at[k], at(0, k), sub_send.at[k], sub_recv.at[k])
        for k in range(1, n_sub)
    ]
    for copy in copies:
        copy.wait_recv()
    summed = jnp.sum(jnp.sum(sub_parts[...], axis=0), axis=1, keepdims=True)
    mom = [jnp.broadcast_to(summed[k : k + 1], (1, 2 * zone_z)) for k in range(2 * CG_ITERS)]

    def inner(left, right, shift):
        acc = None
        for i, a in enumerate(left):
            for j, b in enumerate(right):
                term = a * b * mom[i + j + shift]
                acc = term if acc is None else acc + term
        return acc

    def combine(left, right, factor):
        out = []
        for k in range(max(len(left), len(right))):
            if k >= len(right):
                out.append(left[k])
            elif k >= len(left):
                out.append(factor * right[k])
            else:
                out.append(left[k] + factor * right[k])
        return out

    one = jnp.ones((1, 2 * zone_z), jnp.float32)
    nil = jnp.zeros((1, 2 * zone_z), jnp.float32)
    answer, rest, direction = [], [one], [one]
    norm = mom[0]
    for sweep in range(CG_ITERS):
        step = norm / inner(direction, direction, 1)
        answer = combine(answer, direction, step)
        rest = combine(rest, [nil] + direction, -step)
        if sweep + 1 < CG_ITERS:
            norm_next = inner(rest, rest, 0)
            direction = combine(rest, direction, norm_next / norm)
            norm = norm_next
    for c in range(3):
        for x in range(node_x):
            basis = [total[k, c, x * pad_y : x * pad_y + node_y, :] for k in range(ROUNDS)]
            accel[c, x] = sum(answer[k] * basis[k] for k in range(CG_ITERS))
            residual[c, x] = sum(rest[k] * basis[k] for k in range(ROUNDS))
    for copy in sends:
        copy.wait_send()


def per_device(
    velocity, displacement, energy, rho_weight, mass_share, energy_share, material_id, mix_mask
):
    n_dom, n_sub = lax.axis_size("dom"), lax.axis_size("sub")
    zone_x, zone_y, zone_z = energy.shape[1:]
    node_x, node_y = 2 * zone_x + 1, 2 * zone_y + 1
    pad_x, pad_y = round_up(node_x, 8), round_up(node_y, 8)
    lanes = 4 * zone_z
    plane, wide, tile = node_x * pad_y, 9 * zone_x * zone_y, zone_x * zone_y
    rows_part = plane + 2 * pad_x
    dims = (n_dom, n_sub, zone_x, zone_y, zone_z, pad_x, pad_y, lanes)

    z_value = depth_matrix(value_one, zone_z, lanes)
    z_slope = depth_matrix(slope_one, zone_z, lanes)
    xy = [
        plane_matrix(first, second, zone_x, zone_y, pad_y)
        for first, second in ((value_one, value_one), (slope_one, value_one), (value_one, slope_one))
    ]
    xy_t = [with_faces(table, zone_x, zone_y, pad_y, pad_x) for table in xy]
    weights = np.zeros((9, tile, 4, zone_z), np.float32)
    for a in range(3):
        for b in range(3):
            for q in range(3):
                weights[a * 3 + b, :, q] = quad_one[a] * quad_one[b] * quad_one[q]
    tables = (
        split_table(z_value, 0),
        split_table(z_slope, 0),
        split_table(z_value.T, 0),
        split_table(np.concatenate([z_value.T, z_slope.T], 0), 0),
        split_table(xy[0], 1),
        split_table(np.concatenate([xy[1], xy[2]], 0), 1),
        split_table(xy_t[0], 1),
        split_table(np.concatenate([xy_t[1], xy_t[2]], 1), 1),
        weights.reshape(wide, lanes),
    )
    f32 = jnp.float32
    vmem = pl.BlockSpec(memory_space=pltpu.VMEM)
    return pl.pallas_call(
        functools.partial(kernel, dims),
        out_shape=(
            jax.ShapeDtypeStruct(velocity.shape, f32),
            jax.ShapeDtypeStruct(velocity.shape, f32),
            jax.ShapeDtypeStruct(energy.shape, f32),
        ),
        in_specs=[vmem] * (8 + len(tables)),
        out_specs=(vmem,) * 3,
        scratch_shapes=[
            pltpu.VMEM((2, 3, plane, 2 * zone_z), f32),
            pltpu.VMEM((wide, lanes), f32),
            pltpu.VMEM((3 * MATS + 8, tile, 2 * zone_z), f32),
            pltpu.VMEM((3, wide, 3 * lanes), f32),
            pltpu.VMEM((3, wide, 3 * lanes), f32),
            pltpu.VMEM((ROUNDS, 3, rows_part, 2 * zone_z), f32),
            pltpu.VMEM((ROUNDS, 3, plane, 2 * zone_z), f32),
            pltpu.VMEM((ROUNDS, 2, 3, pad_y, 2 * zone_z), f32),
            pltpu.VMEM((ROUNDS, 2, 3, pad_x, 2 * zone_z), f32),
            pltpu.VMEM((ROUNDS, 4, 3, pad_x, 2 * zone_z), f32),
            pltpu.VMEM((n_dom, 8, 2 * zone_z), f32),
            pltpu.VMEM((n_sub, 8, 2 * zone_z), f32),
            pltpu.SemaphoreType.DMA((ROUNDS, 8)),
            pltpu.SemaphoreType.DMA((ROUNDS, 8)),
            pltpu.SemaphoreType.DMA((n_dom,)),
            pltpu.SemaphoreType.DMA((n_dom,)),
            pltpu.SemaphoreType.DMA((n_sub,)),
            pltpu.SemaphoreType.DMA((n_sub,)),
        ],
        compiler_params=pltpu.CompilerParams(
            collective_id=0, has_side_effects=True, vmem_limit_bytes=32 * 2**20
        ),
    )(
        velocity,
        displacement,
        energy,
        rho_weight,
        mass_share,
        energy_share,
        material_id,
        mix_mask,
        *[jnp.asarray(table) for table in tables],
    )


def solution(mesh):
    blocks = P(None, "dom", "sub", None)
    return jax.shard_map(
        per_device,
        mesh=mesh,
        in_specs=(blocks,) * 6 + (P("dom", "sub", None), blocks),
        out_specs=(blocks,) * 3,
        check_vma=False,
    )
```

time: 235 us -> 49.4 us (0.21)
  blocking collectives: 115 us -> 0 us
  waiting for transfers between devices: 36.1 us -> 0 us
  Pallas kernels: 0 us -> 34.2 us
  local copies, waits for them, and re-layouts: 34.3 us -> 13.9 us
  starting transfers between devices: 12.6 us -> 0 us
  between operations: 13.2 us -> 0.71 us
  matrix products: 12.2 us -> 0 us
  other arithmetic: 10.3 us -> 0 us
    psum x3 -> x0, blocking collectives: 115 us -> none  [inner_pair(): lax.psum((jnp.sum(owned_left * owned_left), jnp.sum(owned_left * owned_ri...]
    ppermute x16 -> x0, waiting for transfers between devices: 36.1 us -> none  [the longest x8 27.8 us: extended(): lax.ppermute(lax.slice_in_dim(block, block.shape[dim] - width, None, axis...]
    pallas_call x0 -> x1, Pallas kernels: none -> 34.2 us  [per_device(): pl.pallas_call(functools.partial(kernel, dims), out_shape=(jax.ShapeDtype...]
    slice x163 -> x0, local copies, waits for them, and re-layouts: 27.4 us -> none  [the longest x135 26.6 us: zone_corners(): by_depth[shift_z]]
    ppermute x16 -> x0, starting transfers between devices: 12.6 us -> none  [the longest x8 8.82 us: extended(): lax.ppermute(lax.slice_in_dim(block, 0, width, axis=dim), axis, backward)]
    dot_general x21 -> x0, matrix products: 12.2 us -> none  [the longest x5 3.59 us: zone_corners(): by_depth = jnp.einsum('cxyk,ksz->scxyz', nodes_in, table, precision=highest)]
    unnamed x161 -> x33, local copies, waits for them, and re-layouts: 4.53 us -> 12.5 us
    reduce_sum x10 -> x0, other arithmetic: 7.63 us -> none  [the longest x4 4 us: zone_force(): fraction = grown_part / jnp.sum(grown_part, 0, keepdims=True)]
  transfers between devices with their start and end apart: 16 -> 0, of which waited for: 14 -> 0; matrix products, arithmetic and copies ran while one was open for 1% -> 0% of each run, Pallas kernels for 0% -> 0%
where the time goes in v1:
time: 49.4 us; the launch traced here: 48.8 us
  Pallas kernels  34.2 us (69%)
  local copies, waits for them, and re-layouts  13.9 us (28%)
  between operations  0.71 us (1%)
    pallas_call x1, Pallas kernels, per_device(): pl.pallas_call(functools.partial(kernel, dims), out_shape=(jax.ShapeDtype...  34.2 us
    unnamed x33, local copies, waits for them, and re-layouts  12.5 us
    pallas_call x2, local copies, waits for them, and re-layouts, per_device(): pl.pallas_call(functools.partial(kernel, dims), out_shape=(jax.ShapeDtype...  1.35 us

profile of v1, /device:TPU:0, one launch (start us, length us, event | category | flops | bytes accessed | tf_op | source)
XLA Modules:
  0.0 48.8 jit_solution(9835261172229499052)
XLA Ops:
  0.6 0.0 copy-start
  0.6 1.0 %copy.20.velocity = f32[3,5,9,128]{3,2,1,0:T(8,128)S(1)} copy(f32[3,5,9,128]{3,0,2,1:T(4,128)} %param.17) | data formatting | bytes 138240 | tf_op args[0]
  1.6 0.0 copy-start.9
  1.6 0.0 copy-start.14
  1.6 0.9 %copy.21.displacement = f32[3,5,9,128]{3,2,1,0:T(8,128)S(1)} copy(f32[3,5,9,128]{3,0,2,1:T(4,128)} %param.18) | data formatting | bytes 138240 | tf_op args[1]
  2.5 0.0 copy-done
  2.6 0.0 copy-done.9
  2.6 0.0 copy-done.14
  2.6 0.0 copy-start.1
  2.6 0.9 %copy-done.1 = bf16[768,128]{1,0:T(8,128)(2,1)S(1)} copy-done((bf16[768,128]{1,0:T(8,128)(2,1)S(1)}, bf16[768,128]{1,0:T(8,128)(2,1)}, u32[]{:S(2)}) %copy-start.1) | copy-done | bytes 196632
  3.5 0.0 copy-start.2
  3.5 0.9 %copy-done.2 = bf16[384,256]{1,0:T(8,128)(2,1)S(1)} copy-done((bf16[384,256]{1,0:T(8,128)(2,1)S(1)}, bf16[384,256]{1,0:T(8,128)(2,1)}, u32[]{:S(2)}) %copy-start.2) | copy-done | bytes 196632
  4.4 0.0 copy-start.3
  4.4 0.9 %copy-done.3 = bf16[384,256]{1,0:T(8,128)(2,1)S(1)} copy-done((bf16[384,256]{1,0:T(8,128)(2,1)S(1)}, bf16[384,256]{1,0:T(8,128)(2,1)}, u32[]{:S(2)}) %copy-start.3) | copy-done | bytes 196632
  5.4 0.0 copy-start.4
  5.4 0.9 %copy-done.4 = f32[27,2,4,64]{3,2,1,0:T(4,128)S(1)} copy-done((f32[27,2,4,64]{3,2,1,0:T(4,128)S(1)}, f32[27,2,4,64]{3,2,1,0:T(4,128)}, u32[]{:S(2)}) %copy-start.4) | copy-done | bytes 55320
  6.3 0.0 copy-start.5
  6.3 0.9 %copy-done.5 = bf16[96,432]{1,0:T(8,128)(2,1)S(1)} copy-done((bf16[96,432]{1,0:T(8,128)(2,1)S(1)}, bf16[96,432]{1,0:T(8,128)(2,1)}, u32[]{:S(2)}) %copy-start.5) | copy-done | bytes 82968
  7.2 0.0 copy-start.6
  7.2 0.9 %copy-done.6 = f32[72,256]{1,0:T(8,128)S(1)} copy-done((f32[72,256]{1,0:T(8,128)S(1)}, f32[72,256]{1,0:T(8,128)}, u32[]{:S(2)}) %copy-start.6) | copy-done | bytes 73752
  8.0 0.0 copy-start.7
  8.0 0.9 %copy-done.7 = bf16[144,240]{1,0:T(8,128)(2,1)S(1)} copy-done((bf16[144,240]{1,0:T(8,128)(2,1)S(1)}, bf16[144,240]{1,0:T(8,128)(2,1)}, u32[]{:S(2)}) %copy-start.7) | copy-done | bytes 69144
  8.9 0.0 copy-start.8
  8.9 0.8 %copy-done.8 = bf16[96,216]{1,0:T(8,128)(2,1)S(1)} copy-done((bf16[96,216]{1,0:T(8,128)(2,1)S(1)}, bf16[96,216]{1,0:T(8,128)(2,1)}, u32[]{:S(2)}) %copy-start.8) | copy-done | bytes 41496
  9.7 0.8 %copy-done.10 = f32[8,2,4,64]{3,2,1,0:T(4,128)S(1)} copy-done((f32[8,2,4,64]{3,2,1,0:T(4,128)S(1)}, f32[8,2,4,64]{3,2,1,0:T(4,128)}, u32[]{:S(2)}) %copy-start.10) | copy-done | bytes 16408
  10.5 0.7 %copy-done.11 = f32[4,2,4,64]{3,2,1,0:T(4,128)S(1)} copy-done((f32[4,2,4,64]{3,2,1,0:T(4,128)S(1)}, f32[4,2,4,64]{3,2,1,0:T(4,128)}, u32[]{:S(2)}) %copy-start.11) | copy-done | bytes 8216
  11.2 0.7 %copy-done.12 = f32[4,2,4,64]{3,2,1,0:T(4,128)S(1)} copy-done((f32[4,2,4,64]{3,2,1,0:T(4,128)S(1)}, f32[4,2,4,64]{3,2,1,0:T(4,128)}, u32[]{:S(2)}) %copy-start.12) | copy-done | bytes 8216
  11.9 0.7 %copy-done.13 = s32[4,2,4,64]{3,2,1,0:T(4,128)S(1)} copy-done((s32[4,2,4,64]{3,2,1,0:T(4,128)S(1)}, s32[4,2,4,64]{3,2,1,0:T(4,128)}, u32[]{:S(2)}) %copy-start.13) | copy-done | bytes 8216
  12.6 34.2 %shard_map.184 = (f32[3,5,9,128]{3,2,1,0:T(8,128)S(1)}, f32[3,5,9,128]{3,2,1,0:T(8,128)S(1)}, f32[8,2,4,64]{3,2,1,0:T(4,128)S(1)}) custom-call(f32[3,5,9,128]{3,2,1,0:T(8,128)S(1)} %copy.20.velocity, f32[3,5,9,128]{3,2,1,0:T(8,128)S(1)} %copy.21.displacement, f32[8,2,4,64]{3,2,1,0:T(4,128)S(1)} %copy-done.10, f32[27,2,4,64]{3,2,1,0:T(4,128)S(1)} %copy-done.4, ...), custom_call_target="tpu_custom_call" | custom-call | tf_op jit(solution)/shard_map/pallas_call | solution.py:499
  46.8 0.7 %copy.22 = f32[3,5,9,128]{3,0,2,1:T(4,128)} copy(f32[3,5,9,128]{3,2,1,0:T(8,128)S(1)} %get-tuple-element.3) | data formatting | bytes 138240 | tf_op jit(solution)/shard_map/pallas_call | solution.py:499
  47.5 0.7 %copy.23 = f32[3,5,9,128]{3,0,2,1:T(4,128)} copy(f32[3,5,9,128]{3,2,1,0:T(8,128)S(1)} %get-tuple-element.4) | data formatting | bytes 138240 | tf_op jit(solution)/shard_map/pallas_call | solution.py:499
  48.2 0.6 %copy.25 = f32[8,2,4,64]{3,2,1,0:T(4,128)} copy(f32[8,2,4,64]{3,2,1,0:T(4,128)S(1)} %get-tuple-element.11) | data formatting | bytes 32768
  (4 shorter events, 0.0 us)
Async XLA Ops:
  0.6 1.9 %copy-start = (bf16[1536,128]{1,0:T(8,128)(2,1)S(1)}, bf16[1536,128]{1,0:T(8,128)(2,1)}, u32[]{:S(2)}) copy-start(bf16[1536,128]{1,0:T(8,128)(2,1)} %constant.21.clone.depth_both_t) | copy-start | bytes 1179652
  1.6 1.0 %copy-start.9 = (bf16[72,240]{1,0:T(8,128)(2,1)S(1)}, bf16[72,240]{1,0:T(8,128)(2,1)}, u32[]{:S(2)}) copy-start(bf16[72,240]{1,0:T(8,128)(2,1)} %constant.22.clone.plane_value) | copy-start | bytes 103684
  1.6 1.0 %copy-start.14 = (s32[2,4,64]{2,1,0:T(4,128)S(1)}, s32[2,4,64]{2,1,0:T(4,128)}, u32[]{:S(2)}) copy-start(s32[2,4,64]{2,1,0:T(4,128)} %material_id.1) | copy-start | bytes 6148
  2.6 0.9 %copy-start.1 = (bf16[768,128]{1,0:T(8,128)(2,1)S(1)}, bf16[768,128]{1,0:T(8,128)(2,1)}, u32[]{:S(2)}) copy-start(bf16[768,128]{1,0:T(8,128)(2,1)} %constant.20.clone.depth_value_t) | copy-start | bytes 589828
  3.5 0.9 %copy-start.2 = (bf16[384,256]{1,0:T(8,128)(2,1)S(1)}, bf16[384,256]{1,0:T(8,128)(2,1)}, u32[]{:S(2)}) copy-start(bf16[384,256]{1,0:T(8,128)(2,1)} %constant.19.clone.depth_slope) | copy-start | bytes 589828
  4.4 0.9 %copy-start.3 = (bf16[384,256]{1,0:T(8,128)(2,1)S(1)}, bf16[384,256]{1,0:T(8,128)(2,1)}, u32[]{:S(2)}) copy-start(bf16[384,256]{1,0:T(8,128)(2,1)} %constant.18.clone.depth_value) | copy-start | bytes 589828
  5.4 0.9 %copy-start.4 = (f32[27,2,4,64]{3,2,1,0:T(4,128)S(1)}, f32[27,2,4,64]{3,2,1,0:T(4,128)}, u32[]{:S(2)}) copy-start(f32[27,2,4,64]{3,2,1,0:T(4,128)} %rho_weight.1) | copy-start | bytes 165892
  6.3 0.9 %copy-start.5 = (bf16[96,432]{1,0:T(8,128)(2,1)S(1)}, bf16[96,432]{1,0:T(8,128)(2,1)}, u32[]{:S(2)}) copy-start(bf16[96,432]{1,0:T(8,128)(2,1)} %constant.25.clone.plane_slopes_t) | copy-start | bytes 248836
  7.2 0.9 %copy-start.6 = (f32[72,256]{1,0:T(8,128)S(1)}, f32[72,256]{1,0:T(8,128)}, u32[]{:S(2)}) copy-start(f32[72,256]{1,0:T(8,128)} %constant.26.clone.weight_table) | copy-start | bytes 221188
  8.0 0.9 %copy-start.7 = (bf16[144,240]{1,0:T(8,128)(2,1)S(1)}, bf16[144,240]{1,0:T(8,128)(2,1)}, u32[]{:S(2)}) copy-start(bf16[144,240]{1,0:T(8,128)(2,1)} %constant.23.clone.plane_slopes) | copy-start | bytes 207364
  8.9 0.8 %copy-start.8 = (bf16[96,216]{1,0:T(8,128)(2,1)S(1)}, bf16[96,216]{1,0:T(8,128)(2,1)}, u32[]{:S(2)}) copy-start(bf16[96,216]{1,0:T(8,128)(2,1)} %constant.24.clone.plane_value_t) | copy-start | bytes 124420
  9.7 0.8 %copy-start.10 = (f32[8,2,4,64]{3,2,1,0:T(4,128)S(1)}, f32[8,2,4,64]{3,2,1,0:T(4,128)}, u32[]{:S(2)}) copy-start(f32[8,2,4,64]{3,2,1,0:T(4,128)} %energy.1) | copy-start | bytes 49156
  10.5 0.7 %copy-start.11 = (f32[4,2,4,64]{3,2,1,0:T(4,128)S(1)}, f32[4,2,4,64]{3,2,1,0:T(4,128)}, u32[]{:S(2)}) copy-start(f32[4,2,4,64]{3,2,1,0:T(4,128)} %mass_share.1) | copy-start | bytes 24580
  11.2 0.7 %copy-start.12 = (f32[4,2,4,64]{3,2,1,0:T(4,128)S(1)}, f32[4,2,4,64]{3,2,1,0:T(4,128)}, u32[]{:S(2)}) copy-start(f32[4,2,4,64]{3,2,1,0:T(4,128)} %energy_share.1) | copy-start | bytes 24580
  11.9 0.7 %copy-start.13 = (s32[4,2,4,64]{3,2,1,0:T(4,128)S(1)}, s32[4,2,4,64]{3,2,1,0:T(4,128)}, u32[]{:S(2)}) copy-start(s32[4,2,4,64]{3,2,1,0:T(4,128)} %mix_mask.1) | copy-start | bytes 24580

commit v2 on v1

--- a/solution.py
+++ b/solution.py
@@ -15,6 +15,7 @@
 EQ_ITERS = 4
 CG_ITERS = 3
 ROUNDS = CG_ITERS + 1
+N_INPUTS = 17
 
 gammas = (1.4, 1.67, 2.0, 3.0)
 cold_terms = (0.3, 1.2, 0.6, 2.4)
@@ -67,15 +68,6 @@
     return table
 
 
-def with_faces(table, zone_x, zone_y, pad_y, pad_x):
-    rows = table.T
-    faces = np.zeros((2, pad_x, rows.shape[1]))
-    for x in range(2 * zone_x + 1):
-        faces[0, x] = rows[x * pad_y]
-        faces[1, x] = rows[x * pad_y + 2 * zone_y]
-    return np.concatenate([rows, faces[0], faces[1]], 0)
-
-
 def split_lanes(x):
     high = x.astype(jnp.bfloat16)
     low = (x - high.astype(jnp.float32)).astype(jnp.bfloat16)
@@ -101,26 +93,38 @@
 
 def kernel(
     dims,
-    velocity,
+    *refs,
+):
+    outer, refs = refs[:N_INPUTS], refs[N_INPUTS:]
+    outputs, refs = refs[:3], refs[3:]
+    inner, refs = refs[:N_INPUTS], refs[N_INPUTS:]
+    body(dims, outer, *inner, *outputs, *refs)
+
+
+def body(
+    dims,
+    outer,
     displacement,
+    depth_value,
+    depth_slope,
+    plane_slopes,
+    plane_value,
+    material_id,
+    mix_mask,
+    mass_share,
+    energy_share,
     energy,
     rho_weight,
-    mass_share,
-    energy_share,
-    material_id,
-    mix_mask,
-    depth_value,
-    depth_slope,
+    weight_table,
+    plane_slopes_t,
+    plane_value_t,
+    depth_both_t,
+    velocity,
     depth_value_t,
-    depth_both_t,
-    plane_value,
-    plane_slopes,
-    plane_value_t,
-    plane_slopes_t,
-    weight_table,
     accel,
     residual,
     energy_rate,
+    load_sem,
     field,
     rho,
     zone_in,
@@ -128,6 +132,8 @@
     stress,
     part,
     total,
+    side_y,
+    side_corner,
     face_x,
     face_y,
     corner,
@@ -157,10 +163,37 @@
     for other in others:
         pl.semaphore_signal(barrier, inc=1, device_id=other, device_id_type=MESH)
 
+    def gradients(which):
+        source = split_lanes(field[which].reshape(3 * plane, 2 * zone_z))
+        by_value = split_rows(lanes_of(product(source, depth_value[...]), plane))
+        by_slope = split_rows(lanes_of(product(source, depth_slope[...]), plane))
+        along_xy = product(plane_slopes[...], by_value)
+        along_z = product(plane_value[...], by_slope)
+        jac[0] = along_xy[:wide]
+        jac[1] = along_xy[wide:]
+        jac[2] = along_z
+
+    inner = (
+        displacement, depth_value, depth_slope, plane_slopes, plane_value, material_id, mix_mask,
+        mass_share, energy_share, energy, rho_weight, weight_table, plane_slopes_t, plane_value_t,
+        depth_both_t, velocity, depth_value_t,
+    )
+    loads = [pltpu.make_async_copy(a, b, load_sem.at[k]) for k, (a, b) in enumerate(zip(outer, inner))]
+    for load in loads:
+        load.start()
     field[...] = jnp.zeros_like(field)
-    for x in range(node_x):
-        field[0, :, x * pad_y : x * pad_y + node_y, :] = displacement[:, x]
-        field[1, :, x * pad_y : x * pad_y + node_y, :] = velocity[:, x]
+    for load in loads[:5]:
+        load.wait()
+
+    def unpack(which, source):
+        for x in range(node_x):
+            for c in range(3):
+                field[which, c, x * pad_y : x * pad_y + node_y, :] = source[x, :, c, :]
+
+    unpack(0, displacement)
+    gradients(0)
+    for load in loads[5:]:
+        load.wait()
     for t in range(9):
         for q in range(4):
             for x in range(zone_x):
@@ -178,18 +211,6 @@
                 zone_in[2 * MATS + m, rows, cols] = energy_share[m, x]
             for j in range(8):
                 zone_in[3 * MATS + j, rows, cols] = energy[j, x]
-
-    def gradients(which):
-        source = split_lanes(field[which].reshape(3 * plane, 2 * zone_z))
-        by_value = split_rows(lanes_of(product(source, depth_value[...]), plane))
-        by_slope = split_rows(lanes_of(product(source, depth_slope[...]), plane))
-        along_xy = product(plane_slopes[...], by_value)
-        along_z = product(plane_value[...], by_slope)
-        jac[0] = along_xy[:wide]
-        jac[1] = along_xy[wide:]
-        jac[2] = along_z
-
-    gradients(0)
 
     present = [zone_in[m] for m in range(MATS)]
     weighted = [present[m] * zone_in[MATS + m] for m in range(MATS)]
@@ -274,11 +295,42 @@
         sends.append(copy)
         return copy
 
+    last = node_x - 1
+
     def start_halo(turn):
+        for k in range(2):
+            row = k * (node_y - 1)
+            for x in range(node_x):
+                for c in range(3):
+                    line = part[turn, c, x * pad_y + row : x * pad_y + row + 1, :]
+                    side_y[turn, k, x, c] = line
+                    if x == 0:
+                        side_corner[turn, k, c] = line
+                    if x == last:
+                        side_corner[turn, 2 + k, c] = line
         copies = []
-        faces_at = (plane, plane + pad_x)
+        for k, (dx, dy) in enumerate(corners):
+            copies.append(
+                send(
+                    side_corner.at[turn, k],
+                    corner.at[turn, k],
+                    at(dx, dy),
+                    halo_send.at[turn, 4 + k],
+                    halo_recv.at[turn, 4 + k],
+                )
+            )
+        for k, dy in enumerate((-1, 1)):
+            copies.append(
+                send(
+                    side_y.at[turn, k],
+                    face_y.at[turn, k],
+                    at(0, dy),
+                    halo_send.at[turn, 2 + k],
+                    halo_recv.at[turn, 2 + k],
+                )
+            )
         for k, dx in enumerate((-1, 1)):
-            first = 0 if dx < 0 else (node_x - 1) * pad_y
+            first = 0 if dx < 0 else last * pad_y
             copies.append(
                 send(
                     part.at[turn, :, pl.ds(first, pad_y), :],
@@ -288,48 +340,28 @@
                     halo_recv.at[turn, k],
                 )
             )
-        for k, dy in enumerate((-1, 1)):
-            copies.append(
-                send(
-                    part.at[turn, :, pl.ds(faces_at[k], pad_x), :],
-                    face_y.at[turn, k],
-                    at(0, dy),
-                    halo_send.at[turn, 2 + k],
-                    halo_recv.at[turn, 2 + k],
-                )
-            )
-        for k, (dx, dy) in enumerate(corners):
-            copies.append(
-                send(
-                    part.at[turn, :, pl.ds(faces_at[0 if dy < 0 else 1], pad_x), :],
-                    corner.at[turn, k],
-                    at(dx, dy),
-                    halo_send.at[turn, 4 + k],
-                    halo_recv.at[turn, 4 + k],
-                )
-            )
         return copies
 
-    row_at = lax.broadcasted_iota(jnp.int32, (3, pad_y, 2 * zone_z), 1)
+    row_at = lax.broadcasted_iota(jnp.int32, (pad_y, 2 * zone_z), 0)
 
     def finish_halo(turn, copies):
         for copy in copies:
             copy.wait_recv()
-        last = node_x - 1
         for x in range(node_x):
-            block = part[turn, :, x * pad_y : (x + 1) * pad_y, :]
-            low = face_y[turn, 1, :, x : x + 1, :]
-            high = face_y[turn, 0, :, x : x + 1, :]
-            if x == 0:
-                block = block + face_x[turn, 1]
-                low = low + corner[turn, 3, :, last : last + 1, :]
-                high = high + corner[turn, 2, :, last : last + 1, :]
-            if x == last:
-                block = block + face_x[turn, 0]
-                low = low + corner[turn, 1, :, 0:1, :]
-                high = high + corner[turn, 0, :, 0:1, :]
-            block = block + jnp.where(row_at == 0, low, jnp.where(row_at == node_y - 1, high, 0.0))
-            total[turn, :, x * pad_y : (x + 1) * pad_y, :] = block
+            for c in range(3):
+                block = part[turn, c, x * pad_y : (x + 1) * pad_y, :]
+                low = face_y[turn, 1, x, c]
+                high = face_y[turn, 0, x, c]
+                if x == 0:
+                    block = block + face_x[turn, 1, c]
+                    low = low + corner[turn, 3, c]
+                    high = high + corner[turn, 2, c]
+                if x == last:
+                    block = block + face_x[turn, 0, c]
+                    low = low + corner[turn, 1, c]
+                    high = high + corner[turn, 0, c]
+                block = block + jnp.where(row_at == 0, low, jnp.where(row_at == node_y - 1, high, 0.0))
+                total[turn, c, x * pad_y : (x + 1) * pad_y, :] = block
 
     def owned(turn):
         return [
@@ -338,24 +370,36 @@
             for x in range(2 * zone_x)
         ]
 
-    def moment(left, right):
-        terms = [a * b for a, b in zip(owned(left), owned(right))]
+    def tree(terms):
         while len(terms) > 1:
             terms = [sum(terms[k : k + 2]) for k in range(0, len(terms), 2)]
         return jnp.sum(terms[0], axis=0, keepdims=True)
+
+    def square(turn):
+        return tree([a * a for a in owned(turn)])
+
+    def energy_of(at_points, scaled):
+        both = at_points * scaled
+        return tree(
+            [
+                both[t * tile : (t + 1) * tile, k * 2 * zone_z : (k + 1) * 2 * zone_z]
+                for t in range(9)
+                for k in range(3 * lanes // (2 * zone_z))
+            ]
+        )
 
     side_xy = product(
         plane_slopes_t[...],
         split_rows(jnp.concatenate([stress[0], stress[1]], axis=0)),
     )
     side_z = product(plane_value_t[...], split_rows(stress[2]))
-    rows_part = plane + 2 * pad_x
     both = jnp.concatenate([rows_of(side_xy, lanes), rows_of(side_z, lanes)], axis=1)
-    part[0] = product(split_lanes(both), depth_both_t[...]).reshape(3, rows_part, 2 * zone_z)
+    part[0] = product(split_lanes(both), depth_both_t[...]).reshape(3, plane, 2 * zone_z)
     pl.semaphore_wait(barrier, len(others))
     copies = start_halo(0)
 
     mass_weight = weight_table[...] * rho[...]
+    unpack(1, velocity)
     gradients(1)
     work = jnp.zeros((wide, lanes), jnp.float32)
     for c in range(3):
@@ -385,36 +429,38 @@
             energy_rate[j, x] = rate[x * zone_y : (x + 1) * zone_y, :zone_z]
 
     finish_halo(0, copies)
-    moments = [moment(0, 0)]
+    moments = []
     weight_three = jnp.concatenate([mass_weight] * 3, axis=1)
     for turn in range(1, ROUNDS):
         source = split_lanes(total[turn - 1].reshape(3 * plane, 2 * zone_z))
         nodes = split_rows(lanes_of(product(source, depth_value[...]), plane))
-        at_points = product(plane_value[...], nodes) * weight_three
-        back = product(plane_value_t[...], split_rows(at_points))
+        at_points = product(plane_value[...], nodes)
+        scaled = at_points * weight_three
+        if turn == ROUNDS - 1:
+            moments += [square(turn - 1), energy_of(at_points, scaled)]
+            fill = jnp.zeros((8 - len(moments), 2 * zone_z), jnp.float32)
+            dom_parts[0] = jnp.concatenate(moments + [fill], axis=0)
+            dom_copies = [
+                send(dom_parts.at[0], dom_parts.at[k], at(k, 0), dom_send.at[k], dom_recv.at[k])
+                for k in range(1, n_dom)
+            ]
+        back = product(plane_value_t[...], split_rows(scaled))
         part[turn] = product(split_lanes(rows_of(back, lanes)), depth_value_t[...]).reshape(
-            3, rows_part, 2 * zone_z
+            3, plane, 2 * zone_z
         )
         copies = start_halo(turn)
-        if turn > 1:
-            moments += [moment(turn - 2, turn - 1), moment(turn - 1, turn - 1)]
-        finish_halo(turn, copies)
-    moments.append(moment(ROUNDS - 2, ROUNDS - 1))
-
-    fill = jnp.zeros((8 - len(moments), 2 * zone_z), jnp.float32)
-    dom_parts[0] = jnp.concatenate(moments + [fill], axis=0)
-    copies = [
-        send(dom_parts.at[0], dom_parts.at[k], at(k, 0), dom_send.at[k], dom_recv.at[k])
-        for k in range(1, n_dom)
-    ]
-    for copy in copies:
+        if turn < ROUNDS - 1:
+            moments += [square(turn - 1), energy_of(at_points, scaled)]
+            finish_halo(turn, copies)
+    for copy in dom_copies:
         copy.wait_recv()
     sub_parts[0] = jnp.sum(dom_parts[...], axis=0)
-    copies = [
+    sub_copies = [
         send(sub_parts.at[0], sub_parts.at[k], at(0, k), sub_send.at[k], sub_recv.at[k])
         for k in range(1, n_sub)
     ]
-    for copy in copies:
+    finish_halo(ROUNDS - 1, copies)
+    for copy in sub_copies:
         copy.wait_recv()
     summed = jnp.sum(jnp.sum(sub_parts[...], axis=0), axis=1, keepdims=True)
     mom = [jnp.broadcast_to(summed[k : k + 1], (1, 2 * zone_z)) for k in range(2 * CG_ITERS)]
@@ -453,8 +499,8 @@
     for c in range(3):
         for x in range(node_x):
             basis = [total[k, c, x * pad_y : x * pad_y + node_y, :] for k in range(ROUNDS)]
-            accel[c, x] = sum(answer[k] * basis[k] for k in range(CG_ITERS))
-            residual[c, x] = sum(rest[k] * basis[k] for k in range(ROUNDS))
+            accel[x, :, c, :] = sum(answer[k] * basis[k] for k in range(CG_ITERS))
+            residual[x, :, c, :] = sum(rest[k] * basis[k] for k in range(ROUNDS))
     for copy in sends:
         copy.wait_send()
 
@@ -468,7 +514,6 @@
     pad_x, pad_y = round_up(node_x, 8), round_up(node_y, 8)
     lanes = 4 * zone_z
     plane, wide, tile = node_x * pad_y, 9 * zone_x * zone_y, zone_x * zone_y
-    rows_part = plane + 2 * pad_x
     dims = (n_dom, n_sub, zone_x, zone_y, zone_z, pad_x, pad_y, lanes)
 
     z_value = depth_matrix(value_one, zone_z, lanes)
@@ -477,45 +522,56 @@
         plane_matrix(first, second, zone_x, zone_y, pad_y)
         for first, second in ((value_one, value_one), (slope_one, value_one), (value_one, slope_one))
     ]
-    xy_t = [with_faces(table, zone_x, zone_y, pad_y, pad_x) for table in xy]
+    xy_t = [table.T for table in xy]
     weights = np.zeros((9, tile, 4, zone_z), np.float32)
     for a in range(3):
         for b in range(3):
             for q in range(3):
                 weights[a * 3 + b, :, q] = quad_one[a] * quad_one[b] * quad_one[q]
-    tables = (
+    order = (1, 2, 0, 3)
+    inputs = (
+        jnp.transpose(displacement, order),
         split_table(z_value, 0),
         split_table(z_slope, 0),
+        split_table(np.concatenate([xy[1], xy[2]], 0), 1),
+        split_table(xy[0], 1),
+        material_id,
+        mix_mask,
+        mass_share,
+        energy_share,
+        energy,
+        rho_weight,
+        weights.reshape(wide, lanes),
+        split_table(np.concatenate([xy_t[1], xy_t[2]], 1), 1),
+        split_table(xy_t[0], 1),
+        split_table(np.concatenate([z_value.T, z_slope.T], 0), 0),
+        jnp.transpose(velocity, order),
         split_table(z_value.T, 0),
-        split_table(np.concatenate([z_value.T, z_slope.T], 0), 0),
-        split_table(xy[0], 1),
-        split_table(np.concatenate([xy[1], xy[2]], 0), 1),
-        split_table(xy_t[0], 1),
-        split_table(np.concatenate([xy_t[1], xy_t[2]], 1), 1),
-        weights.reshape(wide, lanes),
     )
+    inputs = [jnp.asarray(array) for array in inputs]
     f32 = jnp.float32
     vmem = pl.BlockSpec(memory_space=pltpu.VMEM)
-    return pl.pallas_call(
+    nodes_out = jax.ShapeDtypeStruct((node_x, node_y, 3, 2 * zone_z), f32)
+    accel, residual, energy_rate = pl.pallas_call(
         functools.partial(kernel, dims),
-        out_shape=(
-            jax.ShapeDtypeStruct(velocity.shape, f32),
-            jax.ShapeDtypeStruct(velocity.shape, f32),
-            jax.ShapeDtypeStruct(energy.shape, f32),
-        ),
-        in_specs=[vmem] * (8 + len(tables)),
+        out_shape=(nodes_out, nodes_out, jax.ShapeDtypeStruct(energy.shape, f32)),
+        in_specs=[pl.BlockSpec(memory_space=pltpu.HBM)] * N_INPUTS,
         out_specs=(vmem,) * 3,
-        scratch_shapes=[
+        scratch_shapes=[pltpu.VMEM(array.shape, array.dtype) for array in inputs]
+        + [
+            pltpu.SemaphoreType.DMA((N_INPUTS,)),
             pltpu.VMEM((2, 3, plane, 2 * zone_z), f32),
             pltpu.VMEM((wide, lanes), f32),
             pltpu.VMEM((3 * MATS + 8, tile, 2 * zone_z), f32),
             pltpu.VMEM((3, wide, 3 * lanes), f32),
             pltpu.VMEM((3, wide, 3 * lanes), f32),
-            pltpu.VMEM((ROUNDS, 3, rows_part, 2 * zone_z), f32),
             pltpu.VMEM((ROUNDS, 3, plane, 2 * zone_z), f32),
+            pltpu.VMEM((ROUNDS, 3, plane, 2 * zone_z), f32),
+            pltpu.VMEM((ROUNDS, 2, node_x, 3, 1, 2 * zone_z), f32),
+            pltpu.VMEM((ROUNDS, 4, 3, 1, 2 * zone_z), f32),
             pltpu.VMEM((ROUNDS, 2, 3, pad_y, 2 * zone_z), f32),
-            pltpu.VMEM((ROUNDS, 2, 3, pad_x, 2 * zone_z), f32),
-            pltpu.VMEM((ROUNDS, 4, 3, pad_x, 2 * zone_z), f32),
+            pltpu.VMEM((ROUNDS, 2, node_x, 3, 1, 2 * zone_z), f32),
+            pltpu.VMEM((ROUNDS, 4, 3, 1, 2 * zone_z), f32),
             pltpu.VMEM((n_dom, 8, 2 * zone_z), f32),
             pltpu.VMEM((n_sub, 8, 2 * zone_z), f32),
             pltpu.SemaphoreType.DMA((ROUNDS, 8)),
@@ -526,19 +582,11 @@
             pltpu.SemaphoreType.DMA((n_sub,)),
         ],
         compiler_params=pltpu.CompilerParams(
-            collective_id=0, has_side_effects=True, vmem_limit_bytes=32 * 2**20
+            collective_id=0, has_side_effects=True, vmem_limit_bytes=60 * 2**20
         ),
-    )(
-        velocity,
-        displacement,
-        energy,
-        rho_weight,
-        mass_share,
-        energy_share,
-        material_id,
-        mix_mask,
-        *[jnp.asarray(table) for table in tables],
-    )
+    )(*inputs)
+    back = (2, 0, 1, 3)
+    return jnp.transpose(accel, back), jnp.transpose(residual, back), energy_rate
 
 
 def solution(mesh):

time: 49.4 us -> 32.5 us (0.66)
  local copies, waits for them, and re-layouts: 13.9 us -> 2.95 us
  Pallas kernels: 34.2 us -> 28.7 us
    unnamed x33 -> x7, local copies, waits for them, and re-layouts: 12.5 us -> 2.95 us
    pallas_call x1, Pallas kernels: 34.2 us -> 28.7 us  [per_device(): pl.pallas_call(functools.partial(kernel, dims), out_shape=(nodes_out, nod...]
    pallas_call x2 -> x0, local copies, waits for them, and re-layouts: 1.35 us -> none  [per_device(): pl.pallas_call(functools.partial(kernel, dims), out_shape=(jax.ShapeDtype...]
where the time goes in v2:
time: 32.5 us; the launch traced here: 32.3 us
  Pallas kernels  28.7 us (88%)
  local copies, waits for them, and re-layouts  2.95 us (9%)
  between operations  0.65 us (2%)
    pallas_call x1, Pallas kernels, per_device(): pl.pallas_call(functools.partial(kernel, dims), out_shape=(nodes_out, nod...  28.7 us
    unnamed x7, local copies, waits for them, and re-layouts  2.95 us

profile of v2, /device:TPU:0, one launch (start us, length us, event | category | flops | bytes accessed | tf_op | source)
XLA Modules:
  0.0 32.3 jit_solution(14522207843027954589)
XLA Ops:
  0.6 28.7 %shard_map.184 = (f32[5,9,3,128]{3,2,1,0:T(4,128)}, f32[5,9,3,128]{3,2,1,0:T(4,128)}, f32[8,2,4,64]{3,2,1,0:T(4,128)}) custom-call(f32[5,9,3,128]{3,2,1,0:T(4,128)} %bitcast.4, bf16[384,256]{1,0:T(8,128)(2,1)} %constant.18.clone.refs_1_, bf16[384,256]{1,0:T(8,128)(2,1)} %constant.19.clone.refs_2_, bf16[144,240]{1,0:T(8,128)(2,1)} %constant.20.clone.refs_3_, ...), custom_call_target="tpu_custom_call" | custom-call | tf_op jit(solution)/shard_map/pallas_call | solution.py:555
  29.3 0.0 copy-start
  29.3 1.6 %copy.23 = f32[3,5,9,128]{3,0,2,1:T(4,128)} copy(f32[3,5,9,128]{3,0,2,1:T(4,128)} %bitcast.7) | data formatting | bytes 138240
  30.9 0.0 copy-done
  30.9 0.0 copy-start.1
  30.9 0.6 %copy.24 = f32[3,5,9,128]{3,0,2,1:T(4,128)} copy(f32[3,5,9,128]{3,0,2,1:T(4,128)S(1)} %bitcast.6) | data formatting | bytes 138240
  31.5 0.1 copy-done.1
  31.7 0.6 %copy.25 = f32[8,2,4,64]{3,2,1,0:T(4,128)} copy(f32[8,2,4,64]{3,2,1,0:T(4,128)S(1)} %copy-done.1) | data formatting | bytes 32768
Async XLA Ops:
  29.3 1.6 %copy-start = (f32[5,9,3,128]{3,2,1,0:T(4,128)S(1)}, f32[5,9,3,128]{3,2,1,0:T(4,128)}, u32[]{:S(2)}) copy-start(f32[5,9,3,128]{3,2,1,0:T(4,128)} %get-tuple-element.7) | copy-start | bytes 207364
  30.9 0.8 %copy-start.1 = (f32[8,2,4,64]{3,2,1,0:T(4,128)S(1)}, f32[8,2,4,64]{3,2,1,0:T(4,128)}, u32[]{:S(2)}) copy-start(f32[8,2,4,64]{3,2,1,0:T(4,128)} %get-tuple-element.14) | copy-start | bytes 49156

commit v3 on v2

--- a/solution.py
+++ b/solution.py
@@ -121,8 +121,8 @@
     depth_both_t,
     velocity,
     depth_value_t,
-    accel,
-    residual,
+    total,
+    factors,
     energy_rate,
     load_sem,
     field,
@@ -131,7 +131,6 @@
     jac,
     stress,
     part,
-    total,
     side_y,
     side_corner,
     face_x,
@@ -496,13 +495,29 @@
             norm_next = inner(rest, rest, 0)
             direction = combine(rest, direction, norm_next / norm)
             norm = norm_next
-    for c in range(3):
-        for x in range(node_x):
-            basis = [total[k, c, x * pad_y : x * pad_y + node_y, :] for k in range(ROUNDS)]
-            accel[x, :, c, :] = sum(answer[k] * basis[k] for k in range(CG_ITERS))
-            residual[x, :, c, :] = sum(rest[k] * basis[k] for k in range(ROUNDS))
+    for k, factor in enumerate(answer + rest):
+        factors[k] = factor
     for copy in sends:
         copy.wait_send()
+
+
+def combine_kernel(node_y, pad_y, total, factors, rate, accel, residual, energy_rate, one, two, sem):
+    rate_copy = pltpu.make_async_copy(rate, energy_rate, sem.at[0])
+    rate_copy.start()
+    for k, (spot, out, first, count) in enumerate(
+        ((one, accel, 0, CG_ITERS), (two, residual, CG_ITERS, ROUNDS))
+    ):
+        for x in range(one.shape[0]):
+            for c in range(3):
+                terms = [
+                    factors[first + i] * total[i, c, x * pad_y : x * pad_y + node_y, :]
+                    for i in range(count)
+                ]
+                spot[x, :, c, :] = sum(terms[1:], terms[0])
+        pltpu.make_async_copy(spot, out, sem.at[1 + k]).start()
+    rate_copy.wait()
+    for k, (spot, out) in enumerate(((one, accel), (two, residual))):
+        pltpu.make_async_copy(spot, out, sem.at[1 + k]).wait()
 
 
 def per_device(
@@ -548,13 +563,18 @@
         jnp.transpose(velocity, order),
         split_table(z_value.T, 0),
     )
-    inputs = [jnp.asarray(array) for array in inputs]
+    inputs = [pltpu.with_memory_space_constraint(jnp.asarray(array), pltpu.HBM) for array in inputs]
     f32 = jnp.float32
     vmem = pl.BlockSpec(memory_space=pltpu.VMEM)
     nodes_out = jax.ShapeDtypeStruct((node_x, node_y, 3, 2 * zone_z), f32)
-    accel, residual, energy_rate = pl.pallas_call(
+    rate_out = jax.ShapeDtypeStruct(energy.shape, f32)
+    total, factors, rate = pl.pallas_call(
         functools.partial(kernel, dims),
-        out_shape=(nodes_out, nodes_out, jax.ShapeDtypeStruct(energy.shape, f32)),
+        out_shape=(
+            jax.ShapeDtypeStruct((ROUNDS, 3, plane, 2 * zone_z), f32),
+            jax.ShapeDtypeStruct((CG_ITERS + ROUNDS, 1, 2 * zone_z), f32),
+            rate_out,
+        ),
         in_specs=[pl.BlockSpec(memory_space=pltpu.HBM)] * N_INPUTS,
         out_specs=(vmem,) * 3,
         scratch_shapes=[pltpu.VMEM(array.shape, array.dtype) for array in inputs]
@@ -565,7 +585,6 @@
             pltpu.VMEM((3 * MATS + 8, tile, 2 * zone_z), f32),
             pltpu.VMEM((3, wide, 3 * lanes), f32),
             pltpu.VMEM((3, wide, 3 * lanes), f32),
-            pltpu.VMEM((ROUNDS, 3, plane, 2 * zone_z), f32),
             pltpu.VMEM((ROUNDS, 3, plane, 2 * zone_z), f32),
             pltpu.VMEM((ROUNDS, 2, node_x, 3, 1, 2 * zone_z), f32),
             pltpu.VMEM((ROUNDS, 4, 3, 1, 2 * zone_z), f32),
@@ -582,9 +601,22 @@
             pltpu.SemaphoreType.DMA((n_sub,)),
         ],
         compiler_params=pltpu.CompilerParams(
-            collective_id=0, has_side_effects=True, vmem_limit_bytes=60 * 2**20
+            collective_id=0, has_side_effects=True, vmem_limit_bytes=48 * 2**20
         ),
     )(*inputs)
+    hbm = pl.BlockSpec(memory_space=pltpu.HBM)
+    accel, residual, energy_rate = pl.pallas_call(
+        functools.partial(combine_kernel, node_y, pad_y),
+        out_shape=(nodes_out, nodes_out, rate_out),
+        in_specs=[vmem] * 3,
+        out_specs=(hbm,) * 3,
+        scratch_shapes=[
+            pltpu.VMEM(nodes_out.shape, f32),
+            pltpu.VMEM(nodes_out.shape, f32),
+            pltpu.SemaphoreType.DMA((3,)),
+        ],
+        compiler_params=pltpu.CompilerParams(vmem_limit_bytes=8 * 2**20),
+    )(total, factors, rate)
     back = (2, 0, 1, 3)
     return jnp.transpose(accel, back), jnp.transpose(residual, back), energy_rate
 

time: 32.5 us -> 29.5 us (0.908)
  local copies, waits for them, and re-layouts: 2.95 us -> 0 us
    unnamed x7 -> x0, local copies, waits for them, and re-layouts: 2.95 us -> none
    pallas_call x1 -> x2, Pallas kernels: 28.7 us -> 28.7 us  [the longest x1 27.9 us: per_device(): pl.pallas_call(functools.partial(kernel, dims), out_shape=(jax.ShapeDtype...]
where the time goes in v3:
time: 29.5 us; the launch traced here: 29.3 us
  Pallas kernels  28.7 us (97%)
  between operations  0.64 us (2%)
    pallas_call x1, Pallas kernels, per_device(): pl.pallas_call(functools.partial(kernel, dims), out_shape=(jax.ShapeDtype...  27.9 us
    pallas_call x1, Pallas kernels, per_device(): pl.pallas_call(functools.partial(combine_kernel, node_y, pad_y), out_shap...  0.78 us

profile of v3, /device:TPU:0, one launch (start us, length us, event | category | flops | bytes accessed | tf_op | source)
XLA Modules:
  0.0 29.3 jit_solution(14902244684768170062)
XLA Ops:
  0.6 27.9 %shard_map.184 = (f32[4,3,80,128]{3,2,1,0:T(8,128)S(1)}, f32[7,1,128]{2,1,0:T(1,128)S(1)}, f32[8,2,4,64]{3,2,1,0:T(4,128)S(1)}) custom-call(f32[5,9,3,128]{3,2,1,0:T(4,128)} %bitcast.4, bf16[384,256]{1,0:T(8,128)(2,1)} %constant.18.clone.refs_1_, bf16[384,256]{1,0:T(8,128)(2,1)} %constant.19.clone.refs_2_, bf16[144,240]{1,0:T(8,128)(2,1)} %constant.20.clone.refs_3_, ...), custom_call_target="tpu_custom_call" | custom-call | tf_op jit(solution)/shard_map/pallas_call | solution.py:571
  28.5 0.8 %shard_map.185 = (f32[5,9,3,128]{3,2,1,0:T(4,128)}, f32[5,9,3,128]{3,2,1,0:T(4,128)}, f32[8,2,4,64]{3,2,1,0:T(4,128)}) custom-call(f32[4,3,80,128]{3,2,1,0:T(8,128)S(1)} %get-tuple-element.9.total, f32[7,1,128]{2,1,0:T(1,128)S(1)} %get-tuple-element.10.factors, f32[8,2,4,64]{3,2,1,0:T(4,128)S(1)} %get-tuple-element.11.rate), custom_call_target="tpu_custom_call" | custom-call | tf_op jit(solution)/shard_map/pallas_call | solution.py:608

commit v4 on v3

--- a/solution.py
+++ b/solution.py
@@ -15,7 +15,7 @@
 EQ_ITERS = 4
 CG_ITERS = 3
 ROUNDS = CG_ITERS + 1
-N_INPUTS = 17
+N_INPUTS = 18
 
 gammas = (1.4, 1.67, 2.0, 3.0)
 cold_terms = (0.3, 1.2, 0.6, 2.4)
@@ -121,11 +121,13 @@
     depth_both_t,
     velocity,
     depth_value_t,
+    plane_sides,
     total,
     factors,
     energy_rate,
     load_sem,
     field,
+    rows_y,
     rho,
     zone_in,
     jac,
@@ -156,8 +158,11 @@
         return (lax.rem(me_dom + shift_dom + n_dom, n_dom), lax.rem(me_sub + shift_sub + n_sub, n_sub))
 
     corners = [(-1, -1), (-1, 1), (1, -1), (1, 1)]
-    others = [at(k, 0) for k in range(1, n_dom)] + [at(0, k) for k in range(1, n_sub)]
-    others += [at(dx, dy) for dx, dy in corners]
+    along_dom = [at(k, 0) for k in range(1, n_dom)]
+    along_sub = [at(0, k) for k in range(1, n_sub)]
+    diagonal = [at(dx, dy) for dx, dy in corners]
+    beside_x, beside_y = (along_dom[-1], along_dom[0]), (along_sub[-1], along_sub[0])
+    others = along_dom + along_sub + diagonal
     barrier = pltpu.get_barrier_semaphore()
     for other in others:
         pl.semaphore_signal(barrier, inc=1, device_id=other, device_id_type=MESH)
@@ -175,12 +180,13 @@
     inner = (
         displacement, depth_value, depth_slope, plane_slopes, plane_value, material_id, mix_mask,
         mass_share, energy_share, energy, rho_weight, weight_table, plane_slopes_t, plane_value_t,
-        depth_both_t, velocity, depth_value_t,
+        depth_both_t, velocity, depth_value_t, plane_sides,
     )
     loads = [pltpu.make_async_copy(a, b, load_sem.at[k]) for k, (a, b) in enumerate(zip(outer, inner))]
     for load in loads:
         load.start()
     field[...] = jnp.zeros_like(field)
+    rows_y[...] = jnp.zeros_like(rows_y)
     for load in loads[:5]:
         load.wait()
 
@@ -313,7 +319,7 @@
                 send(
                     side_corner.at[turn, k],
                     corner.at[turn, k],
-                    at(dx, dy),
+                    diagonal[k],
                     halo_send.at[turn, 4 + k],
                     halo_recv.at[turn, 4 + k],
                 )
@@ -323,7 +329,7 @@
                 send(
                     side_y.at[turn, k],
                     face_y.at[turn, k],
-                    at(0, dy),
+                    beside_y[k],
                     halo_send.at[turn, 2 + k],
                     halo_recv.at[turn, 2 + k],
                 )
@@ -334,33 +340,42 @@
                 send(
                     part.at[turn, :, pl.ds(first, pad_y), :],
                     face_x.at[turn, k],
-                    at(dx, 0),
+                    beside_x[k],
                     halo_send.at[turn, k],
                     halo_recv.at[turn, k],
                 )
             )
         return copies
 
-    row_at = lax.broadcasted_iota(jnp.int32, (pad_y, 2 * zone_z), 0)
-
-    def finish_halo(turn, copies):
-        for copy in copies:
+    def finish_x(turn, copies):
+        for copy in copies[6:]:
+            copy.wait_recv()
+        for x in range(node_x):
+            block = part[turn, :, x * pad_y : (x + 1) * pad_y, :]
+            if x == 0:
+                block = block + face_x[turn, 1]
+            if x == last:
+                block = block + face_x[turn, 0]
+            total[turn, :, x * pad_y : (x + 1) * pad_y, :] = block
+
+    def finish_y(turn, copies):
+        for copy in copies[:6]:
             copy.wait_recv()
         for x in range(node_x):
             for c in range(3):
-                block = part[turn, c, x * pad_y : (x + 1) * pad_y, :]
-                low = face_y[turn, 1, x, c]
-                high = face_y[turn, 0, x, c]
-                if x == 0:
-                    block = block + face_x[turn, 1, c]
-                    low = low + corner[turn, 3, c]
-                    high = high + corner[turn, 2, c]
-                if x == last:
-                    block = block + face_x[turn, 0, c]
-                    low = low + corner[turn, 1, c]
-                    high = high + corner[turn, 0, c]
-                block = block + jnp.where(row_at == 0, low, jnp.where(row_at == node_y - 1, high, 0.0))
-                total[turn, c, x * pad_y : (x + 1) * pad_y, :] = block
+                for k in range(2):
+                    line = face_y[turn, 1 - k, x, c]
+                    if x == 0:
+                        line = line + corner[turn, 3 - k, c]
+                    if x == last:
+                        line = line + corner[turn, 1 - k, c]
+                    rows_y[c, k * pad_x + x : k * pad_x + x + 1, :] = line
+
+    def add_y(turn):
+        for x in range(node_x):
+            for k in range(2):
+                row = x * pad_y + k * (node_y - 1)
+                total[turn, :, row : row + 1, :] += rows_y[:, k * pad_x + x : k * pad_x + x + 1, :]
 
     def owned(turn):
         return [
@@ -427,20 +442,25 @@
         for x in range(zone_x):
             energy_rate[j, x] = rate[x * zone_y : (x + 1) * zone_y, :zone_z]
 
-    finish_halo(0, copies)
     moments = []
     weight_three = jnp.concatenate([mass_weight] * 3, axis=1)
     for turn in range(1, ROUNDS):
+        finish_x(turn - 1, copies)
         source = split_lanes(total[turn - 1].reshape(3 * plane, 2 * zone_z))
         nodes = split_rows(lanes_of(product(source, depth_value[...]), plane))
         at_points = product(plane_value[...], nodes)
+        finish_y(turn - 1, copies)
+        source = split_lanes(rows_y[...].reshape(6 * pad_x, 2 * zone_z))
+        nodes = split_rows(lanes_of(product(source, depth_value[...]), 2 * pad_x))
+        at_points = at_points + product(plane_sides[...], nodes)
         scaled = at_points * weight_three
         if turn == ROUNDS - 1:
+            add_y(turn - 1)
             moments += [square(turn - 1), energy_of(at_points, scaled)]
             fill = jnp.zeros((8 - len(moments), 2 * zone_z), jnp.float32)
             dom_parts[0] = jnp.concatenate(moments + [fill], axis=0)
             dom_copies = [
-                send(dom_parts.at[0], dom_parts.at[k], at(k, 0), dom_send.at[k], dom_recv.at[k])
+                send(dom_parts.at[0], dom_parts.at[k], along_dom[k - 1], dom_send.at[k], dom_recv.at[k])
                 for k in range(1, n_dom)
             ]
         back = product(plane_value_t[...], split_rows(scaled))
@@ -449,16 +469,18 @@
         )
         copies = start_halo(turn)
         if turn < ROUNDS - 1:
+            add_y(turn - 1)
             moments += [square(turn - 1), energy_of(at_points, scaled)]
-            finish_halo(turn, copies)
     for copy in dom_copies:
         copy.wait_recv()
     sub_parts[0] = jnp.sum(dom_parts[...], axis=0)
     sub_copies = [
-        send(sub_parts.at[0], sub_parts.at[k], at(0, k), sub_send.at[k], sub_recv.at[k])
+        send(sub_parts.at[0], sub_parts.at[k], along_sub[k - 1], sub_send.at[k], sub_recv.at[k])
         for k in range(1, n_sub)
     ]
-    finish_halo(ROUNDS - 1, copies)
+    finish_x(ROUNDS - 1, copies)
+    finish_y(ROUNDS - 1, copies)
+    add_y(ROUNDS - 1)
     for copy in sub_copies:
         copy.wait_recv()
     summed = jnp.sum(jnp.sum(sub_parts[...], axis=0), axis=1, keepdims=True)
@@ -538,6 +560,10 @@
         for first, second in ((value_one, value_one), (slope_one, value_one), (value_one, slope_one))
     ]
     xy_t = [table.T for table in xy]
+    sides = np.zeros((wide, 2 * pad_x))
+    for x in range(node_x):
+        sides[:, x] = xy[0][:, x * pad_y]
+        sides[:, pad_x + x] = xy[0][:, x * pad_y + 2 * zone_y]
     weights = np.zeros((9, tile, 4, zone_z), np.float32)
     for a in range(3):
         for b in range(3):
@@ -562,6 +588,7 @@
         split_table(np.concatenate([z_value.T, z_slope.T], 0), 0),
         jnp.transpose(velocity, order),
         split_table(z_value.T, 0),
+        split_table(sides, 1),
     )
     inputs = [pltpu.with_memory_space_constraint(jnp.asarray(array), pltpu.HBM) for array in inputs]
     f32 = jnp.float32
@@ -581,6 +608,7 @@
         + [
             pltpu.SemaphoreType.DMA((N_INPUTS,)),
             pltpu.VMEM((2, 3, plane, 2 * zone_z), f32),
+            pltpu.VMEM((3, 2 * pad_x, 2 * zone_z), f32),
             pltpu.VMEM((wide, lanes), f32),
             pltpu.VMEM((3 * MATS + 8, tile, 2 * zone_z), f32),
             pltpu.VMEM((3, wide, 3 * lanes), f32),

time: 29.5 us -> 29.4 us (level)
  no operation moved by 1% of the time
where the time goes in v4:
time: 29.4 us; the launch traced here: 29.3 us
  Pallas kernels  28.6 us (97%)
  between operations  0.64 us (2%)
    pallas_call x1, Pallas kernels, per_device(): pl.pallas_call(functools.partial(kernel, dims), out_shape=(jax.ShapeDtype...  27.8 us
    pallas_call x1, Pallas kernels, per_device(): pl.pallas_call(functools.partial(combine_kernel, node_y, pad_y), out_shap...  0.78 us

profile of v4, /device:TPU:0, one launch (start us, length us, event | category | flops | bytes accessed | tf_op | source)
XLA Modules:
  0.0 29.3 jit_solution(1937992733620038842)
XLA Ops:
  0.6 27.8 %shard_map.193 = (f32[4,3,80,128]{3,2,1,0:T(8,128)S(1)}, f32[7,1,128]{2,1,0:T(1,128)S(1)}, f32[8,2,4,64]{3,2,1,0:T(4,128)S(1)}) custom-call(f32[5,9,3,128]{3,2,1,0:T(4,128)} %bitcast.4, bf16[384,256]{1,0:T(8,128)(2,1)} %constant.20.clone.refs_1_, bf16[384,256]{1,0:T(8,128)(2,1)} %constant.21.clone.refs_2_, bf16[144,240]{1,0:T(8,128)(2,1)} %constant.22.clone.refs_3_, ...), custom_call_target="tpu_custom_call" | custom-call | tf_op jit(solution)/shard_map/pallas_call | solution.py:598
  28.5 0.8 %shard_map.194 = (f32[5,9,3,128]{3,2,1,0:T(4,128)}, f32[5,9,3,128]{3,2,1,0:T(4,128)}, f32[8,2,4,64]{3,2,1,0:T(4,128)}) custom-call(f32[4,3,80,128]{3,2,1,0:T(8,128)S(1)} %get-tuple-element.9.total, f32[7,1,128]{2,1,0:T(1,128)S(1)} %get-tuple-element.10.factors, f32[8,2,4,64]{3,2,1,0:T(4,128)S(1)} %get-tuple-element.11.rate), custom_call_target="tpu_custom_call" | custom-call | tf_op jit(solution)/shard_map/pallas_call | solution.py:636

commit v5 on v4

--- a/solution.py
+++ b/solution.py
@@ -413,12 +413,14 @@
     copies = start_halo(0)
 
     mass_weight = weight_table[...] * rho[...]
-    unpack(1, velocity)
-    gradients(1)
-    work = jnp.zeros((wide, lanes), jnp.float32)
-    for c in range(3):
-        for d in range(3):
-            work = work + jac[d, :, c * lanes : (c + 1) * lanes] * stress[d, :, c * lanes : (c + 1) * lanes]
+
+    def contract():
+        work = jnp.zeros((wide, lanes), jnp.float32)
+        for c in range(3):
+            for d in range(3):
+                cols = slice(c * lanes, (c + 1) * lanes)
+                work = work + jac[d, :, cols] * stress[d, :, cols]
+        return work
 
     def to_linear(x):
         results = []
@@ -435,12 +437,13 @@
                     results.append(folded + pltpu.roll(folded, zone_z, 1))
         return results
 
-    rates = to_linear(work)
-    lumped = to_linear(mass_weight)
-    for j in range(8):
-        rate = -rates[j] / lumped[j]
-        for x in range(zone_x):
-            energy_rate[j, x] = rate[x * zone_y : (x + 1) * zone_y, :zone_z]
+    def store_rate():
+        rates = to_linear(contract())
+        lumped = to_linear(mass_weight)
+        for j in range(8):
+            rate = -rates[j] / lumped[j]
+            for x in range(zone_x):
+                energy_rate[j, x] = rate[x * zone_y : (x + 1) * zone_y, :zone_z]
 
     moments = []
     weight_three = jnp.concatenate([mass_weight] * 3, axis=1)
@@ -471,6 +474,11 @@
         if turn < ROUNDS - 1:
             add_y(turn - 1)
             moments += [square(turn - 1), energy_of(at_points, scaled)]
+        if turn == 1:
+            unpack(1, velocity)
+            gradients(1)
+        if turn == 2:
+            store_rate()
     for copy in dom_copies:
         copy.wait_recv()
     sub_parts[0] = jnp.sum(dom_parts[...], axis=0)

time: 29.4 us -> 29.5 us (level)
  no operation moved by 1% of the time
where the time goes in v5:
time: 29.5 us; the launch traced here: 29.3 us
  Pallas kernels  28.7 us (97%)
  between operations  0.64 us (2%)
    pallas_call x1, Pallas kernels, per_device(): pl.pallas_call(functools.partial(kernel, dims), out_shape=(jax.ShapeDtype...  27.9 us
    pallas_call x1, Pallas kernels, per_device(): pl.pallas_call(functools.partial(combine_kernel, node_y, pad_y), out_shap...  0.78 us

profile of v5, /device:TPU:0, one launch (start us, length us, event | category | flops | bytes accessed | tf_op | source)
XLA Modules:
  0.0 29.3 jit_solution(13988192557789404305)
XLA Ops:
  0.6 27.9 %shard_map.193 = (f32[4,3,80,128]{3,2,1,0:T(8,128)S(1)}, f32[7,1,128]{2,1,0:T(1,128)S(1)}, f32[8,2,4,64]{3,2,1,0:T(4,128)S(1)}) custom-call(f32[5,9,3,128]{3,2,1,0:T(4,128)} %bitcast.4, bf16[384,256]{1,0:T(8,128)(2,1)} %constant.20.clone.refs_1_, bf16[384,256]{1,0:T(8,128)(2,1)} %constant.21.clone.refs_2_, bf16[144,240]{1,0:T(8,128)(2,1)} %constant.22.clone.refs_3_, ...), custom_call_target="tpu_custom_call" | custom-call | tf_op jit(solution)/shard_map/pallas_call | solution.py:606
  28.5 0.8 %shard_map.194 = (f32[5,9,3,128]{3,2,1,0:T(4,128)}, f32[5,9,3,128]{3,2,1,0:T(4,128)}, f32[8,2,4,64]{3,2,1,0:T(4,128)}) custom-call(f32[4,3,80,128]{3,2,1,0:T(8,128)S(1)} %get-tuple-element.9.total, f32[7,1,128]{2,1,0:T(1,128)S(1)} %get-tuple-element.10.factors, f32[8,2,4,64]{3,2,1,0:T(4,128)S(1)} %get-tuple-element.11.rate), custom_call_target="tpu_custom_call" | custom-call | tf_op jit(solution)/shard_map/pallas_call | solution.py:644

commit v6 on v5

--- a/solution.py
+++ b/solution.py
@@ -163,9 +163,6 @@
     diagonal = [at(dx, dy) for dx, dy in corners]
     beside_x, beside_y = (along_dom[-1], along_dom[0]), (along_sub[-1], along_sub[0])
     others = along_dom + along_sub + diagonal
-    barrier = pltpu.get_barrier_semaphore()
-    for other in others:
-        pl.semaphore_signal(barrier, inc=1, device_id=other, device_id_type=MESH)
 
     def gradients(which):
         source = split_lanes(field[which].reshape(3 * plane, 2 * zone_z))
@@ -185,17 +182,21 @@
     loads = [pltpu.make_async_copy(a, b, load_sem.at[k]) for k, (a, b) in enumerate(zip(outer, inner))]
     for load in loads:
         load.start()
+    barrier = pltpu.get_barrier_semaphore()
+    for other in others:
+        pl.semaphore_signal(barrier, inc=1, device_id=other, device_id_type=MESH)
     field[...] = jnp.zeros_like(field)
     rows_y[...] = jnp.zeros_like(rows_y)
-    for load in loads[:5]:
-        load.wait()
 
     def unpack(which, source):
         for x in range(node_x):
             for c in range(3):
                 field[which, c, x * pad_y : x * pad_y + node_y, :] = source[x, :, c, :]
 
+    loads[0].wait()
     unpack(0, displacement)
+    for load in loads[1:5]:
+        load.wait()
     gradients(0)
     for load in loads[5:]:
         load.wait()

time: 29.5 us -> 29.5 us (level)
  no operation moved by 1% of the time
where the time goes in v6:
time: 29.5 us; the launch traced here: 29.3 us
  Pallas kernels  28.7 us (97%)
  between operations  0.64 us (2%)
    pallas_call x1, Pallas kernels, per_device(): pl.pallas_call(functools.partial(kernel, dims), out_shape=(jax.ShapeDtype...  27.9 us
    pallas_call x1, Pallas kernels, per_device(): pl.pallas_call(functools.partial(combine_kernel, node_y, pad_y), out_shap...  0.78 us

profile of v6, /device:TPU:0, one launch (start us, length us, event | category | flops | bytes accessed | tf_op | source)
XLA Modules:
  0.0 29.3 jit_solution(8733016859118374013)
XLA Ops:
  0.6 27.9 %shard_map.193 = (f32[4,3,80,128]{3,2,1,0:T(8,128)S(1)}, f32[7,1,128]{2,1,0:T(1,128)S(1)}, f32[8,2,4,64]{3,2,1,0:T(4,128)S(1)}) custom-call(f32[5,9,3,128]{3,2,1,0:T(4,128)} %bitcast.4, bf16[384,256]{1,0:T(8,128)(2,1)} %constant.20.clone.refs_1_, bf16[384,256]{1,0:T(8,128)(2,1)} %constant.21.clone.refs_2_, bf16[144,240]{1,0:T(8,128)(2,1)} %constant.22.clone.refs_3_, ...), custom_call_target="tpu_custom_call" | custom-call | tf_op jit(solution)/shard_map/pallas_call | solution.py:607
  28.6 0.8 %shard_map.194 = (f32[5,9,3,128]{3,2,1,0:T(4,128)}, f32[5,9,3,128]{3,2,1,0:T(4,128)}, f32[8,2,4,64]{3,2,1,0:T(4,128)}) custom-call(f32[4,3,80,128]{3,2,1,0:T(8,128)S(1)} %get-tuple-element.9.total, f32[7,1,128]{2,1,0:T(1,128)S(1)} %get-tuple-element.10.factors, f32[8,2,4,64]{3,2,1,0:T(4,128)S(1)} %get-tuple-element.11.rate), custom_call_target="tpu_custom_call" | custom-call | tf_op jit(solution)/shard_map/pallas_call | solution.py:645
